TPU v7x, 32 devices: a whole 2x2x4 slice. The times are simulated.
32 devices in a mesh: tm: 2 (over x), azim: 16 (over z, y, core).
Axes of the slice: x: 2, y: 2, z: 4, core: 2. Of those that a mesh axis runs over, the one named last changes fastest.
Arguments:
- pressure: bfloat16 [256, 160, 256], P('azim', None, 'tm'), may hold values from -6 to 6
Outputs:
- gram_xx: float32 [128, 2, 256, 256], P('azim', None, 'tm')
- gram_xy: float32 [128, 2, 256, 256], P('azim', None, 'tm')
All inputs are finite; a program needn't handle non-finite values.
Results may differ from a plain program's by a relative error of at most 0.0046.
Values may be sent and summed in bfloat16 or wider, within the bound.
A program may use at most 64 MiB of HBM per device.

v0:
```python
import jax
import jax.numpy as jnp
from jax import lax
from jax.sharding import PartitionSpec as P

THETA = 256
MODES = 128
ROWS = 160


def make_table(parts):
    per_set = MODES // parts
    column = jnp.arange(2 * MODES, dtype=jnp.int32)
    owner = column // (2 * per_set)
    within = column % (2 * per_set)
    imag_flag = within // per_set
    wave = owner * per_set + within % per_set
    angle_idx = jnp.arange(THETA, dtype=jnp.int32)[:, None]
    phase = (angle_idx * wave[None, :] % THETA).astype(jnp.float32) * (2.0 * jnp.pi / THETA)
    scale = THETA ** (-0.5)
    values = jnp.where(imag_flag[None, :] == 1, -jnp.sin(phase), jnp.cos(phase)) * scale
    return values.astype(jnp.bfloat16)


def complex_tiles(left_cat, right, gain):
    width = right.shape[3]
    half = left_cat.shape[2] // 2
    right_cat = jnp.transpose(right, (1, 2, 0, 3)).reshape(
        right.shape[1], right.shape[2], 2 * width
    )
    product = jnp.einsum("jrs,jru->jsu", left_cat, right_cat, preferred_element_type=jnp.float32)
    real = product[:, :half, :width] + product[:, half:, width:]
    imag = product[:, :half, width:] - product[:, half:, :width]
    return jnp.stack([real, imag], axis=1) * gain


def body(pressure):
    parts = lax.axis_size("azim")
    snap_dev = pressure.shape[2]
    table = make_table(parts)
    spectrum = jnp.einsum(
        "art,ac->crt",
        lax.all_to_all(pressure, "azim", split_axis=2, concat_axis=0, tiled=True),
        table,
        preferred_element_type=jnp.float32,
    ).astype(jnp.bfloat16)
    owned = lax.all_to_all(spectrum, "azim", split_axis=0, concat_axis=2, tiled=True)
    modes = owned.reshape(2, owned.shape[0] // 2, owned.shape[1], owned.shape[2])
    per_set = modes.shape[1]
    depth = modes.shape[2]
    gain = ROWS ** (-0.5)
    left_cat = jnp.transpose(modes, (1, 2, 0, 3)).reshape(per_set, depth, 2 * snap_dev)
    limit = (lax.axis_index("tm") + 1) * snap_dev

    def place(tile):
        columns = jnp.arange(tile.shape[3], dtype=jnp.int32)
        tile = jnp.where((columns < limit)[None, None, None, :], tile, jnp.float32(0.0))
        return tile

    heads = lax.all_gather(modes[..., :1], "tm", axis=3, tiled=True)
    heads_next = jnp.concatenate(
        [heads[..., 1:], jnp.zeros(heads.shape[:3] + (1,), jnp.bfloat16)], axis=3
    )
    piece = lax.all_gather(modes, "tm", axis=3, tiled=True)
    last_block = (jnp.int32(0) + piece.shape[3]) // snap_dev - 1
    tail = lax.dynamic_slice_in_dim(heads_next, last_block, 1, 3)
    block_y = jnp.concatenate([piece[..., 1:], tail], axis=3)
    gram_xx = place(complex_tiles(left_cat, piece, gain))
    gram_xy = place(complex_tiles(left_cat, block_y, gain))
    return (gram_xx, gram_xy)


def solution(mesh):
    in_specs = (P("azim", None, "tm"),)
    out_specs = (P("azim", None, "tm", None), P("azim", None, "tm", None))
    return jax.shard_map(body, mesh=mesh, in_specs=in_specs, out_specs=out_specs, check_vma=False)
```

profile of v0, /device:TPU:0, one launch (start us, length us, event | category | flops | bytes accessed | tf_op | source)
XLA Modules:
  0.0 139.6 jit_solution(9113196706345654127)
XLA Ops:
  7.2 2.6 %copy.16 = bf16[16,160,128]{1,0,2:T(8,128)(2,1)} copy(bf16[16,160,128]{2,1,0:T(8,128)(2,1)} %param.1) | data formatting | bytes 1310720 | tf_op args[0]
  9.7 7.4 %all-to-all-start = ((bf16[16,160,128]{1,0,2:T(8,128)(2,1)}), bf16[16,160,128]{1,0,2:T(8,128)(2,1)S(1)}, u32[]{:S(2)}, u32[]{:S(2)}) async-start(bf16[16,160,128]{1,0,2:T(8,128)(2,1)} %copy.16), calls=%async_computation | async-start | bytes 2097152 | tf_op jit(solution)/shard_map/all_to_all | solution.py:43
  17.1 0.0 all-gather.2.cloned.1.call-start
  17.2 22.9 %all-to-all-done = bf16[16,160,128]{1,0,2:T(8,128)(2,1)S(1)} async-done(((bf16[16,160,128]{1,0,2:T(8,128)(2,1)}), bf16[16,160,128]{1,0,2:T(8,128)(2,1)S(1)}, u32[]{:S(2)}, u32[]{:S(2)}) %all-to-all-start) | async-done | bytes 655392 | tf_op jit(solution)/shard_map/all_to_all | solution.py:43
  40.1 0.4 copy.18
  40.5 1.5 %convolution_convert_fusion = bf16[256,160,8]{0,1,2:T(8,128)(2,1)S(1)} fusion(bf16[256,160,8]{1,2,0:T(8,128)(2,1)S(1)} %bitcast.33, s32[256]{0:T(256)S(1)} %fusion.23, pred[256]{0:T(512)(128)(4,1)S(1)} %fusion.25), kind=kOutput, calls=%fused_computation.5 | convolution fusion | flops 169279488 | bytes 1312000 | tf_op jit(solution)/shard_map/art,ac->crt/dot_general | solution.py:41
  42.0 0.9 copy.20
  43.0 31.5 %all_to_all.33 = bf16[256,160,8]{1,2,0:T(8,128)(2,1)S(1)} all-to-all(bf16[256,160,8]{1,2,0:T(8,128)(2,1)S(1)} %copy.20), channel_id=1, replica_groups=mesh['tm'=2,'azim'=16] {'azim'}, dimensions={0} | all-to-all | bytes 1310720 | tf_op jit(solution)/shard_map/all_to_all | solution.py:47
  74.5 1.1 copy.21
  75.6 3.0 %copy.22 = bf16[8,160,2,128]{3,2,1,0:T(2,128)(2,1)S(1)} copy(bf16[8,160,2,128]{1,3,0,2:T(8,128)(2,1)} %bitcast.29) | data formatting | bytes 1310720 | tf_op jit(solution)/shard_map/transpose | solution.py:52
  78.6 0.4 reshape.75
  79.0 30.1 %all-gather.2.cloned.1.call-done = bf16[2,8,160,256]{2,3,1,0:T(8,128)(2,1)} async-done(((bf16[2,8,160,128]{2,3,1,0:T(8,128)(2,1)}), bf16[2,8,160,256]{2,3,1,0:T(8,128)(2,1)}) %all-gather.2.cloned.1.call-update) | async-done | bytes 1310736 | tf_op jit(solution)/shard_map/all_gather | solution.py:64
  109.2 5.1 %copy.23 = bf16[8,160,2,256]{3,2,1,0:T(2,128)(2,1)} copy(bf16[8,160,2,256]{1,3,0,2:T(8,128)(2,1)} %bitcast.30) | data formatting | bytes 2621440 | tf_op jit(solution)/shard_map/transpose | solution.py:28
  114.3 4.4 %reshape.76 = bf16[8,160,512]{2,1,0:T(8,128)(2,1)} reshape(bf16[8,160,2,256]{3,2,1,0:T(2,128)(2,1)} %copy.23) | data formatting | bytes 2621440 | tf_op jit(solution)/shard_map/reshape | solution.py:28
  118.7 1.0 slice.43
  119.6 0.4 pad_bitcast_fusion
  120.1 3.1 %copy.24 = bf16[8,160,2,256]{3,2,1,0:T(2,128)(2,1)} copy(bf16[8,160,2,256]{1,3,0,2:T(8,128)(2,1)S(1)} %pad_bitcast_fusion) | data formatting | bytes 2621440 | tf_op jit(solution)/shard_map/transpose | solution.py:28
  123.2 3.5 %reshape.77 = bf16[8,160,512]{2,1,0:T(8,128)(2,1)S(1)} reshape(bf16[8,160,2,256]{3,2,1,0:T(2,128)(2,1)} %copy.24) | data formatting | bytes 2621440 | tf_op jit(solution)/shard_map/reshape | solution.py:28
  126.7 0.8 fusion.31
  127.5 0.8 fusion.32
  128.4 0.7 fusion.3
  129.1 0.5 fusion.1
  129.6 1.5 %copy.25 = f32[8,2,128,256]{3,2,1,0:T(8,128)} copy(f32[8,2,128,256]{3,2,0,1:T(8,128)S(1)} %get-tuple-element.13) | data formatting | bytes 4194304
  131.2 1.5 %copy.26 = f32[8,2,128,256]{3,2,1,0:T(8,128)} copy(f32[8,2,128,256]{3,2,0,1:T(8,128)S(1)} %get-tuple-element.12) | data formatting | bytes 4194304
  (8 shorter events, 0.0 us)
Async XLA Ops:
  9.7 30.3 %all-to-all-start = ((bf16[16,160,128]{1,0,2:T(8,128)(2,1)}), bf16[16,160,128]{1,0,2:T(8,128)(2,1)S(1)}, u32[]{:S(2)}, u32[]{:S(2)}) async-start(bf16[16,160,128]{1,0,2:T(8,128)(2,1)} %copy.16), calls=%async_computation | async-start | bytes 2097152 | tf_op jit(solution)/shard_map/all_to_all | solution.py:43
  17.1 92.0 %all-gather.2.cloned.1.call-start = ((), (), s32[]{:S(2)}) async-start(), calls=%async_computation.2 | async-start | bytes 3145728 | tf_op jit(solution)/shard_map/all_gather | solution.py:64
  114.3 4.4 %copy-start = (bf16[2,8,160,256]{2,3,1,0:T(8,128)(2,1)S(1)}, bf16[2,8,160,256]{2,3,1,0:T(8,128)(2,1)}, u32[]{:S(2)}) copy-start(bf16[2,8,160,256]{2,3,1,0:T(8,128)(2,1)} %all-gather.2.cloned.1.call-done) | copy-start | bytes 3932164
  123.2 3.5 %copy-start.1 = (bf16[8,160,512]{2,1,0:T(8,128)(2,1)S(1)}, bf16[8,160,512]{2,1,0:T(8,128)(2,1)}, u32[]{:S(2)}) copy-start(bf16[8,160,512]{2,1,0:T(8,128)(2,1)} %reshape.76) | copy-start | bytes 3932164
Sparse Core Ops, SparseCore 0:
  75.7 33.4 all-gather.1
where the time goes:
time: 140 us
  waiting for transfers between devices  53 us (38%)
  blocking collectives  31.5 us (22%)
  local copies, waits for them, and re-layouts  29 us (21%)
  between operations  14.1 us (10%)
  starting transfers between devices  7.43 us (5%)
  matrix products  3.17 us (2%)
    all_to_all x1, blocking collectives, body(): lax.all_to_all(spectrum, 'azim', split_axis=0, concat_axis=2, tiled=True)  31.5 us
    all_gather x1, waiting for transfers between devices, body(): piece = lax.all_gather(modes, 'tm', axis=3, tiled=True)  30.1 us
    all_to_all x1, waiting for transfers between devices, body(): lax.all_to_all(pressure, 'azim', split_axis=2, concat_axis=0, tiled=True)  22.9 us
    transpose x3, local copies, waits for them, and re-layouts, complex_tiles(): jnp.transpose(right, (1, 2, 0, 3))  8.65 us
    reshape x2, local copies, waits for them, and re-layouts, complex_tiles(): jnp.transpose(right, (1, 2, 0, 3))  7.89 us
    all_to_all x1, starting transfers between devices, body(): lax.all_to_all(pressure, 'azim', split_axis=2, concat_axis=0, tiled=True)  7.39 us
    unnamed x7, local copies, waits for them, and re-layouts  5.66 us
    transpose x1, local copies, waits for them, and re-layouts, body(): jnp.transpose(modes, (1, 2, 0, 3)).reshape(per_set, depth, 2 * snap_dev)  2.97 us
  transfers between devices with their start and end apart: 2, of which 2 were waited for; matrix products, arithmetic and copies ran while one was open for 2% of the time, Pallas kernels for 0%

commit v1 on v0

v1 whole, which is shorter than its diff:
```python
import functools

import jax
import jax.numpy as jnp
import ml_dtypes
import numpy as np
from jax import lax
from jax.experimental import pallas as pl
from jax.experimental.pallas import tpu as pltpu
from jax.sharding import PartitionSpec as P

MESH = pl.DeviceIdType.MESH
TILE = 16


def dft_table(theta, parts, group):
    angles = theta // parts
    per_set = theta // 2 // parts
    column = np.arange(theta)
    owner, within = column // (2 * per_set), column % (2 * per_set)
    wave = owner * per_set + within % per_set
    index = (wave[:, None] * np.arange(theta)[None, :]) % theta
    phase = index.astype(np.float32) * np.float32(2.0 * np.pi / theta)
    scale = np.float32(theta ** -0.5)
    imag = (within // per_set == 1)[:, None]
    values = np.where(imag, -np.sin(phase), np.cos(phase)) * scale
    values = values.reshape(parts, 1, 2 * per_set, parts, 1, angles)
    eye = np.eye(group, dtype=np.float32).reshape(1, group, 1, 1, group, 1)
    side = theta * group
    return (values * eye).reshape(side, side).astype(ml_dtypes.bfloat16)


def swap_table(outer, inner):
    row = np.arange(outer * inner)
    source = (row % inner) * outer + row // inner
    return (source[:, None] == row[None, :]).astype(ml_dtypes.bfloat16)


def matmul(a, b):
    return jnp.dot(a, b, preferred_element_type=jnp.float32).astype(jnp.bfloat16)


def exchange_kernel(
    parts, blocks, unit, groups, chunks,
    x_ref, swap_in, swap_out, table, modes_ref,
    pack, rx1, tx, rx2, send1, recv1, send2, recv2, send3, recv3,
):
    me = lax.axis_index("azim")
    tm = lax.axis_index("tm")
    angles, rows, width = x_ref.shape
    blk = unit * groups
    cb = blk // chunks
    per_chunk = groups // chunks
    padded = parts * blk // angles

    barrier = pltpu.get_barrier_semaphore()

    def greet(s, carry):
        pl.semaphore_signal(
            barrier, inc=1, device_id=(tm, lax.rem(me + s, parts)), device_id_type=MESH
        )
        return carry

    lax.fori_loop(1, parts, greet, 0)
    for d in range(1, blocks):
        pl.semaphore_signal(
            barrier, inc=1, device_id=(lax.rem(tm + d, blocks), me), device_id_type=MESH
        )

    step = TILE * angles
    for k in range(padded // TILE):
        if k * TILE < rows:
            part = x_ref[:, k * TILE:(k + 1) * TILE, :].reshape(step, width)
            pack[k * step:(k + 1) * step, :] = matmul(swap_in[...], part)
        else:
            pack[k * step:(k + 1) * step, :] = jnp.zeros((step, width), jnp.bfloat16)

    pl.semaphore_wait(barrier, parts - 1 + blocks - 1)

    def shift(i):
        return 1 + lax.rem(parts // 2 - 1 + i, parts - 1)

    def copy1(c, s):
        to = lax.rem(me + s, parts)
        return pltpu.make_async_remote_copy(
            src_ref=pack.at[pl.ds(pl.multiple_of(to * blk + c * cb, TILE), cb), :],
            dst_ref=rx1.at[me, pl.ds(c * cb, cb), :],
            send_sem=send1.at[c, s],
            recv_sem=recv1.at[c, s],
            device_id=(tm, to),
            device_id_type=MESH,
        )

    def copy2(c, s):
        to = lax.rem(me + s, parts)
        return pltpu.make_async_remote_copy(
            src_ref=tx.at[to, pl.ds(c * cb, cb), :],
            dst_ref=rx2.at[tm, me, pl.ds(c * cb, cb), :],
            send_sem=send2.at[c, s],
            recv_sem=recv2.at[c, s],
            device_id=(tm, to),
            device_id_type=MESH,
        )

    def landed1(c, s):
        source = lax.rem(me + parts - s, parts)
        here = rx1.at[source, pl.ds(c * cb, cb), :]
        return pltpu.make_async_remote_copy(
            src_ref=here, dst_ref=here, send_sem=send1.at[c, s], recv_sem=recv1.at[c, s],
            device_id=(tm, source), device_id_type=MESH,
        )

    def landed2(c, s):
        source = lax.rem(me + parts - s, parts)
        here = rx2.at[tm, source, pl.ds(c * cb, cb), :]
        return pltpu.make_async_remote_copy(
            src_ref=here, dst_ref=here, send_sem=send2.at[c, s], recv_sem=recv2.at[c, s],
            device_id=(tm, source), device_id_type=MESH,
        )

    def copy3(c, source, d):
        here = rx2.at[tm, source, pl.ds(c * cb, cb), :]
        return pltpu.make_async_remote_copy(
            src_ref=here, dst_ref=here,
            send_sem=send3.at[d, c, source], recv_sem=recv3.at[d, c, source],
            device_id=(lax.rem(tm + d, blocks), me), device_id_type=MESH,
        )

    def landed3(c, source, d):
        here = rx2.at[lax.rem(tm + blocks - d, blocks), source, pl.ds(c * cb, cb), :]
        return pltpu.make_async_remote_copy(
            src_ref=here, dst_ref=here,
            send_sem=send3.at[d, c, source], recv_sem=recv3.at[d, c, source],
            device_id=(lax.rem(tm + blocks - d, blocks), me), device_id_type=MESH,
        )

    def guarded(condition, act):
        if blocks == 2:
            act()
        else:
            pl.when(condition)(act)

    def needed_by(d):
        return lax.rem(tm + d, blocks) >= tm - 1

    def needed_from(d):
        return lax.rem(tm + blocks - d, blocks) <= tm + 1

    def loop(body):
        def run(i, carry):
            body(shift(i))
            return carry
        lax.fori_loop(0, parts - 1, run, 0)

    def forward(c, source):
        for d in range(1, blocks):
            guarded(needed_by(d), lambda d=d: copy3(c, source, d).start())

    for c in range(chunks):
        loop(lambda s, c=c: copy1(c, s).start())
    rx1[pl.ds(me, 1)] = pack[pl.ds(pl.multiple_of(me * blk, TILE), blk), :].reshape(1, blk, width)

    for c in range(chunks):
        loop(lambda s, c=c: landed1(c, s).wait_recv())
        for q in range(c * per_chunk, (c + 1) * per_chunk):
            field = rx1[:, q * unit:(q + 1) * unit, :].reshape(parts * unit, width)
            tx[:, q * unit:(q + 1) * unit, :] = matmul(table[...], field).reshape(parts, unit, width)
        loop(lambda s, c=c: copy2(c, s).start())
        rx2[tm, me, c * cb:(c + 1) * cb, :] = tx[me, c * cb:(c + 1) * cb, :]
        forward(c, me)

    for c in range(chunks):
        def pass_on(s, c=c):
            landed2(c, s).wait_recv()
            forward(c, lax.rem(me + parts - s, parts))
        loop(pass_on)

    def regroup(block):
        step_out = TILE * angles
        flat = rx2.at[block].reshape(parts * blk, width)
        for k in range(padded // TILE):
            tile = matmul(swap_out[...], flat[k * step_out:(k + 1) * step_out, :])
            modes_ref[:, k * TILE:(k + 1) * TILE, pl.ds(pl.multiple_of(block * width, width), width)] = (
                tile.reshape(angles, TILE, width)
            )

    regroup(tm)
    for d in range(1, blocks):
        def take(d=d):
            for c in range(chunks):
                def arrive(i, carry, c=c):
                    landed3(c, lax.rem(me + i, parts), d).wait_recv()
                    return carry
                lax.fori_loop(0, parts, arrive, 0)
            regroup(lax.rem(tm + blocks - d, blocks))

        guarded(needed_from(d), take)
        if blocks > 2:
            @pl.when(jnp.logical_not(needed_from(d)))
            def _(d=d):
                other = lax.rem(tm + blocks - d, blocks)
                modes_ref[:, :, pl.ds(pl.multiple_of(other * width, width), width)] = jnp.zeros(
                    (angles, padded, width), jnp.bfloat16
                )

    for c in range(chunks):
        loop(lambda s, c=c: copy1(c, s).wait_send())
        loop(lambda s, c=c: copy2(c, s).wait_send())
        for d in range(1, blocks):
            def sent(d=d, c=c):
                def one(i, carry):
                    copy3(c, i, d).wait_send()
                    return carry
                lax.fori_loop(0, parts, one, 0)
            guarded(needed_by(d), sent)


def gram_kernel(gain, width, modes_ref, xx_ref, xy_ref):
    tm = lax.axis_index("tm")
    count, full = modes_ref.shape[1], modes_ref.shape[3]
    limit = (tm + 1) * width
    columns = lax.broadcasted_iota(jnp.int32, (width, full), 1)
    keep_xx = columns < limit
    keep_xy = columns < jnp.minimum(limit, full - 1)
    own = pl.ds(pl.multiple_of(tm * width, width), width)
    for m in range(count):
        real, imag = modes_ref[0, m], modes_ref[1, m]
        left = jnp.concatenate([modes_ref[0, m, :, own], modes_ref[1, m, :, own]], axis=0)
        for p, right in ((0, [real, imag]), (1, [imag, -real])):
            product = lax.dot_general(
                left, jnp.concatenate(right, axis=0), (((0,), (0,)), ((), ())),
                preferred_element_type=jnp.float32,
            ) * gain
            xx_ref[m, p] = jnp.where(keep_xx, product, 0.0)
            xy_ref[m, p] = jnp.where(keep_xy, pltpu.roll(product, full - 1, 1), 0.0)


def body(parts, blocks, pressure):
    angles, rows, width = pressure.shape
    theta = angles * parts
    per_set = theta // 2 // parts
    group = max(1, TILE // angles)
    unit = group * angles
    groups = -(-rows // (parts * group))
    while parts * groups * group % TILE:
        groups += 1
    chunks = 2 if groups % 2 == 0 else 1
    blk = unit * groups
    padded = parts * groups * group
    full = blocks * width

    vmem = pl.BlockSpec(memory_space=pltpu.VMEM)
    dma = pltpu.SemaphoreType.DMA
    modes = pl.pallas_call(
        functools.partial(exchange_kernel, parts, blocks, unit, groups, chunks),
        out_shape=jax.ShapeDtypeStruct((angles, padded, full), jnp.bfloat16),
        in_specs=[vmem] * 4,
        out_specs=vmem,
        scratch_shapes=[
            pltpu.VMEM((parts * blk, width), jnp.bfloat16),
            pltpu.VMEM((parts, blk, width), jnp.bfloat16),
            pltpu.VMEM((parts, blk, width), jnp.bfloat16),
            pltpu.VMEM((blocks, parts, blk, width), jnp.bfloat16),
            dma((chunks, parts)), dma((chunks, parts)),
            dma((chunks, parts)), dma((chunks, parts)),
            dma((blocks, chunks, parts)), dma((blocks, chunks, parts)),
        ],
        compiler_params=pltpu.CompilerParams(
            collective_id=0, has_side_effects=True, vmem_limit_bytes=48 * 2**20
        ),
        name="exchange",
    )(
        pressure,
        jnp.asarray(swap_table(TILE, angles)),
        jnp.asarray(swap_table(angles, TILE)),
        jnp.asarray(dft_table(theta, parts, group)),
    )
    modes = modes.reshape(2, per_set, padded, full)
    shape = jax.ShapeDtypeStruct((per_set, 2, width, full), jnp.float32)
    out = pl.BlockSpec((1, 2, width, full), lambda i: (i, 0, 0, 0))
    return pl.pallas_call(
        functools.partial(gram_kernel, rows ** -0.5, width),
        grid=(per_set,),
        out_shape=(shape, shape),
        in_specs=[pl.BlockSpec((2, 1, padded, full), lambda i: (0, i, 0, 0))],
        out_specs=(out, out),
        compiler_params=pltpu.CompilerParams(vmem_limit_bytes=48 * 2**20),
        name="grams",
    )(modes)


def solution(mesh):
    parts, blocks = mesh.shape["azim"], mesh.shape["tm"]
    in_specs = (P("azim", None, "tm"),)
    out_specs = (P("azim", None, "tm", None), P("azim", None, "tm", None))
    return jax.shard_map(
        functools.partial(body, parts, blocks),
        mesh=mesh, in_specs=in_specs, out_specs=out_specs, check_vma=False,
    )
```

time: 140 us -> 54.4 us (0.39)
  waiting for transfers between devices: 53 us -> 0 us
  Pallas kernels: 0 us -> 50.7 us
  blocking collectives: 31.5 us -> 0 us
  local copies, waits for them, and re-layouts: 29 us -> 2.89 us
  between operations: 14.1 us -> 0.65 us
  starting transfers between devices: 7.43 us -> 0 us
  matrix products: 3.17 us -> 0 us
    pallas_call x0 -> x2, Pallas kernels: none -> 50.7 us  [the longest x1 45.9 us: body(): pl.pallas_call(functools.partial(exchange_kernel, parts, blocks, unit, gr...]
    all_to_all x1 -> x0, blocking collectives: 31.5 us -> none  [body(): lax.all_to_all(spectrum, 'azim', split_axis=0, concat_axis=2, tiled=True)]
    all_gather x1 -> x0, waiting for transfers between devices: 30.1 us -> none  [body(): piece = lax.all_gather(modes, 'tm', axis=3, tiled=True)]
    all_to_all x1 -> x0, waiting for transfers between devices: 22.9 us -> none  [body(): lax.all_to_all(pressure, 'azim', split_axis=2, concat_axis=0, tiled=True)]
    transpose x4 -> x0, local copies, waits for them, and re-layouts: 11.6 us -> none  [the longest x3 8.65 us: complex_tiles(): jnp.transpose(right, (1, 2, 0, 3))]
    reshape x3 -> x0, local copies, waits for them, and re-layouts: 8.3 us -> none  [the longest x2 7.89 us: complex_tiles(): jnp.transpose(right, (1, 2, 0, 3))]
    all_to_all x1 -> x0, starting transfers between devices: 7.39 us -> none  [body(): lax.all_to_all(pressure, 'azim', split_axis=2, concat_axis=0, tiled=True)]
    dot_general x3 -> x0, matrix products: 3.17 us -> none  [the longest x2 1.66 us: complex_tiles(): jnp.einsum('jrs,jru->jsu', left_cat, right_cat, preferred_element_type=jn...]
  transfers between devices with their start and end apart: 2 -> 0, of which waited for: 2 -> 0; matrix products, arithmetic and copies ran while one was open for 2% -> 0% of each run, Pallas kernels for 0% -> 0%
where the time goes in v1:
time: 54.4 us; the launch traced here: 54.3 us
  Pallas kernels  50.7 us (93%)
  local copies, waits for them, and re-layouts  2.89 us (5%)
  between operations  0.65 us (1%)
    pallas_call x1, Pallas kernels, body(): pl.pallas_call(functools.partial(exchange_kernel, parts, blocks, unit, gr...  45.9 us
    pallas_call x1, Pallas kernels, body(): pl.pallas_call(functools.partial(gram_kernel, rows ** (-0.5), width), gri...  4.78 us
    unnamed x6, local copies, waits for them, and re-layouts  2.89 us

profile of v1, /device:TPU:0, one launch (start us, length us, event | category | flops | bytes accessed | tf_op | source)
XLA Modules:
  0.0 54.3 jit_solution(4369922449997925935)
XLA Ops:
  0.6 0.0 copy-start
  0.6 1.1 %copy-done = bf16[16,160,128]{2,1,0:T(8,128)(2,1)S(1)} copy-done((bf16[16,160,128]{2,1,0:T(8,128)(2,1)S(1)}, bf16[16,160,128]{2,1,0:T(8,128)(2,1)}, u32[]{:S(2)}) %copy-start) | copy-done | bytes 655384
  1.7 0.0 copy-start.1
  1.7 0.9 %copy-done.1 = bf16[256,256]{1,0:T(8,128)(2,1)S(1)} copy-done((bf16[256,256]{1,0:T(8,128)(2,1)S(1)}, bf16[256,256]{1,0:T(8,128)(2,1)}, u32[]{:S(2)}) %copy-start.1) | copy-done | bytes 131096
  2.6 0.0 copy-start.2
  2.6 0.9 %copy-done.2 = bf16[256,256]{1,0:T(8,128)(2,1)S(1)} copy-done((bf16[256,256]{1,0:T(8,128)(2,1)S(1)}, bf16[256,256]{1,0:T(8,128)(2,1)}, u32[]{:S(2)}) %copy-start.2) | copy-done | bytes 131096
  3.5 45.9 %exchange.1 = bf16[16,160,256]{2,1,0:T(8,128)(2,1)S(1)} custom-call(bf16[16,160,128]{2,1,0:T(8,128)(2,1)S(1)} %copy-done, bf16[256,256]{1,0:T(8,128)(2,1)S(1)} %copy-done.1, bf16[256,256]{1,0:T(8,128)(2,1)S(1)} %copy-done.1, bf16[256,256]{1,0:T(8,128)(2,1)S(1)} %copy-done.2), custom_call_target="tpu_custom_call" | custom-call | tf_op jit(solution)/shard_map/exchange/pallas_call | solution.py:254
  49.5 4.8 %grams.1 = (f32[8,2,128,256]{3,2,1,0:T(8,128)}, f32[8,2,128,256]{3,2,1,0:T(8,128)}) custom-call(bf16[2,8,160,256]{3,2,1,0:T(8,128)(2,1)S(1)} %bitcast.1), custom_call_target="tpu_custom_call" | custom-call | tf_op jit(solution)/shard_map/grams/pallas_call | solution.py:281
Async XLA Ops:
  0.6 1.1 %copy-start = (bf16[16,160,128]{2,1,0:T(8,128)(2,1)S(1)}, bf16[16,160,128]{2,1,0:T(8,128)(2,1)}, u32[]{:S(2)}) copy-start(bf16[16,160,128]{2,1,0:T(8,128)(2,1)} %x_ref.1) | copy-start | bytes 1966084
  1.7 0.9 %copy-start.1 = (bf16[256,256]{1,0:T(8,128)(2,1)S(1)}, bf16[256,256]{1,0:T(8,128)(2,1)}, u32[]{:S(2)}) copy-start(bf16[256,256]{1,0:T(8,128)(2,1)} %constant.4.clone.swap_in.swap_out) | copy-start | bytes 393220
  2.6 0.9 %copy-start.2 = (bf16[256,256]{1,0:T(8,128)(2,1)S(1)}, bf16[256,256]{1,0:T(8,128)(2,1)}, u32[]{:S(2)}) copy-start(bf16[256,256]{1,0:T(8,128)(2,1)} %constant.5.clone.table) | copy-start | bytes 393220

commit v2 on v1

--- a/solution.py
+++ b/solution.py
@@ -42,8 +42,9 @@
 
 def exchange_kernel(
     parts, blocks, unit, groups, chunks,
-    x_ref, swap_in, swap_out, table, modes_ref,
-    pack, rx1, tx, rx2, send1, recv1, send2, recv2, send3, recv3,
+    x_hbm, swap_in_hbm, swap_out_hbm, table_hbm, modes_ref,
+    x_ref, swap_in, swap_out, table, pack, rx1, tx, rx2,
+    load, send1, recv1, send2, recv2, send3, recv3,
 ):
     me = lax.axis_index("azim")
     tm = lax.axis_index("tm")
@@ -53,12 +54,27 @@
     per_chunk = groups // chunks
     padded = parts * blk // angles
 
+    loads = [
+        pltpu.make_async_copy(src, dst, load.at[i])
+        for i, (src, dst) in enumerate(
+            ((swap_in_hbm, swap_in), (x_hbm, x_ref), (table_hbm, table), (swap_out_hbm, swap_out))
+        )
+    ]
+    for copy in loads:
+        copy.start()
+
     barrier = pltpu.get_barrier_semaphore()
 
+    def peer(s):
+        other, bit = 0, 1
+        while bit < parts:
+            mine, flip = lax.rem(me // bit, 2), lax.rem(s // bit, 2)
+            other = other + bit * (mine + flip - 2 * mine * flip)
+            bit *= 2
+        return other
+
     def greet(s, carry):
-        pl.semaphore_signal(
-            barrier, inc=1, device_id=(tm, lax.rem(me + s, parts)), device_id_type=MESH
-        )
+        pl.semaphore_signal(barrier, inc=1, device_id=(tm, peer(s)), device_id_type=MESH)
         return carry
 
     lax.fori_loop(1, parts, greet, 0)
@@ -67,6 +83,8 @@
             barrier, inc=1, device_id=(lax.rem(tm + d, blocks), me), device_id_type=MESH
         )
 
+    loads[0].wait()
+    loads[1].wait()
     step = TILE * angles
     for k in range(padded // TILE):
         if k * TILE < rows:
@@ -78,13 +96,14 @@
     pl.semaphore_wait(barrier, parts - 1 + blocks - 1)
 
     def shift(i):
-        return 1 + lax.rem(parts // 2 - 1 + i, parts - 1)
+        odd = lax.rem(i, 2)
+        return i // 2 + odd + (parts // 2) * (1 - odd)
 
     def copy1(c, s):
-        to = lax.rem(me + s, parts)
+        to = peer(s)
         return pltpu.make_async_remote_copy(
             src_ref=pack.at[pl.ds(pl.multiple_of(to * blk + c * cb, TILE), cb), :],
-            dst_ref=rx1.at[me, pl.ds(c * cb, cb), :],
+            dst_ref=rx1.at[c, me],
             send_sem=send1.at[c, s],
             recv_sem=recv1.at[c, s],
             device_id=(tm, to),
@@ -92,10 +111,10 @@
         )
 
     def copy2(c, s):
-        to = lax.rem(me + s, parts)
-        return pltpu.make_async_remote_copy(
-            src_ref=tx.at[to, pl.ds(c * cb, cb), :],
-            dst_ref=rx2.at[tm, me, pl.ds(c * cb, cb), :],
+        to = peer(s)
+        return pltpu.make_async_remote_copy(
+            src_ref=tx.at[c, to],
+            dst_ref=rx2.at[tm, c, me],
             send_sem=send2.at[c, s],
             recv_sem=recv2.at[c, s],
             device_id=(tm, to),
@@ -103,23 +122,23 @@
         )
 
     def landed1(c, s):
-        source = lax.rem(me + parts - s, parts)
-        here = rx1.at[source, pl.ds(c * cb, cb), :]
+        source = peer(s)
+        here = rx1.at[c, source]
         return pltpu.make_async_remote_copy(
             src_ref=here, dst_ref=here, send_sem=send1.at[c, s], recv_sem=recv1.at[c, s],
             device_id=(tm, source), device_id_type=MESH,
         )
 
     def landed2(c, s):
-        source = lax.rem(me + parts - s, parts)
-        here = rx2.at[tm, source, pl.ds(c * cb, cb), :]
+        source = peer(s)
+        here = rx2.at[tm, c, source]
         return pltpu.make_async_remote_copy(
             src_ref=here, dst_ref=here, send_sem=send2.at[c, s], recv_sem=recv2.at[c, s],
             device_id=(tm, source), device_id_type=MESH,
         )
 
     def copy3(c, source, d):
-        here = rx2.at[tm, source, pl.ds(c * cb, cb), :]
+        here = rx2.at[tm, c, source]
         return pltpu.make_async_remote_copy(
             src_ref=here, dst_ref=here,
             send_sem=send3.at[d, c, source], recv_sem=recv3.at[d, c, source],
@@ -127,7 +146,7 @@
         )
 
     def landed3(c, source, d):
-        here = rx2.at[lax.rem(tm + blocks - d, blocks), source, pl.ds(c * cb, cb), :]
+        here = rx2.at[lax.rem(tm + blocks - d, blocks), c, source]
         return pltpu.make_async_remote_copy(
             src_ref=here, dst_ref=here,
             send_sem=send3.at[d, c, source], recv_sem=recv3.at[d, c, source],
@@ -158,41 +177,44 @@
 
     for c in range(chunks):
         loop(lambda s, c=c: copy1(c, s).start())
-    rx1[pl.ds(me, 1)] = pack[pl.ds(pl.multiple_of(me * blk, TILE), blk), :].reshape(1, blk, width)
+        rx1[c, me] = pack[pl.ds(pl.multiple_of(me * blk + c * cb, TILE), cb), :]
+    loads[2].wait()
+    loads[3].wait()
 
     for c in range(chunks):
         loop(lambda s, c=c: landed1(c, s).wait_recv())
-        for q in range(c * per_chunk, (c + 1) * per_chunk):
-            field = rx1[:, q * unit:(q + 1) * unit, :].reshape(parts * unit, width)
-            tx[:, q * unit:(q + 1) * unit, :] = matmul(table[...], field).reshape(parts, unit, width)
+        for q in range(per_chunk):
+            field = rx1[c, :, q * unit:(q + 1) * unit, :].reshape(parts * unit, width)
+            tx[c, :, q * unit:(q + 1) * unit, :] = matmul(table[...], field).reshape(parts, unit, width)
         loop(lambda s, c=c: copy2(c, s).start())
-        rx2[tm, me, c * cb:(c + 1) * cb, :] = tx[me, c * cb:(c + 1) * cb, :]
+        rx2[tm, c, me] = tx[c, me]
         forward(c, me)
+
+    span = padded // chunks
+
+    def regroup(block, c):
+        for k in range(span // TILE):
+            rows_in = rx2.at[block, c].reshape(parts * cb, width)[k * step:(k + 1) * step, :]
+            modes_ref[
+                :, c * span + k * TILE:c * span + (k + 1) * TILE,
+                pl.ds(pl.multiple_of(block * width, width), width),
+            ] = matmul(swap_out[...], rows_in).reshape(angles, TILE, width)
 
     for c in range(chunks):
         def pass_on(s, c=c):
             landed2(c, s).wait_recv()
-            forward(c, lax.rem(me + parts - s, parts))
+            forward(c, peer(s))
         loop(pass_on)
-
-    def regroup(block):
-        step_out = TILE * angles
-        flat = rx2.at[block].reshape(parts * blk, width)
-        for k in range(padded // TILE):
-            tile = matmul(swap_out[...], flat[k * step_out:(k + 1) * step_out, :])
-            modes_ref[:, k * TILE:(k + 1) * TILE, pl.ds(pl.multiple_of(block * width, width), width)] = (
-                tile.reshape(angles, TILE, width)
-            )
-
-    regroup(tm)
+        regroup(tm, c)
+
     for d in range(1, blocks):
         def take(d=d):
             for c in range(chunks):
                 def arrive(i, carry, c=c):
-                    landed3(c, lax.rem(me + i, parts), d).wait_recv()
+                    landed3(c, i, d).wait_recv()
                     return carry
                 lax.fori_loop(0, parts, arrive, 0)
-            regroup(lax.rem(tm + blocks - d, blocks))
+                regroup(lax.rem(tm + blocks - d, blocks), c)
 
         guarded(needed_from(d), take)
         if blocks > 2:
@@ -244,23 +266,30 @@
     groups = -(-rows // (parts * group))
     while parts * groups * group % TILE:
         groups += 1
-    chunks = 2 if groups % 2 == 0 else 1
     blk = unit * groups
     padded = parts * groups * group
+    chunks = 2 if groups % 2 == 0 and padded % (2 * TILE) == 0 else 1
     full = blocks * width
 
+    swap = swap_table(TILE, angles)
+    table = dft_table(theta, parts, group)
     vmem = pl.BlockSpec(memory_space=pltpu.VMEM)
     dma = pltpu.SemaphoreType.DMA
     modes = pl.pallas_call(
         functools.partial(exchange_kernel, parts, blocks, unit, groups, chunks),
         out_shape=jax.ShapeDtypeStruct((angles, padded, full), jnp.bfloat16),
-        in_specs=[vmem] * 4,
+        in_specs=[pl.BlockSpec(memory_space=pltpu.HBM)] * 4,
         out_specs=vmem,
         scratch_shapes=[
+            pltpu.VMEM(pressure.shape, jnp.bfloat16),
+            pltpu.VMEM(swap.shape, jnp.bfloat16),
+            pltpu.VMEM(swap.shape, jnp.bfloat16),
+            pltpu.VMEM(table.shape, jnp.bfloat16),
             pltpu.VMEM((parts * blk, width), jnp.bfloat16),
-            pltpu.VMEM((parts, blk, width), jnp.bfloat16),
-            pltpu.VMEM((parts, blk, width), jnp.bfloat16),
-            pltpu.VMEM((blocks, parts, blk, width), jnp.bfloat16),
+            pltpu.VMEM((chunks, parts, blk // chunks, width), jnp.bfloat16),
+            pltpu.VMEM((chunks, parts, blk // chunks, width), jnp.bfloat16),
+            pltpu.VMEM((blocks, chunks, parts, blk // chunks, width), jnp.bfloat16),
+            dma((4,)),
             dma((chunks, parts)), dma((chunks, parts)),
             dma((chunks, parts)), dma((chunks, parts)),
             dma((blocks, chunks, parts)), dma((blocks, chunks, parts)),
@@ -271,9 +300,9 @@
         name="exchange",
     )(
         pressure,
-        jnp.asarray(swap_table(TILE, angles)),
+        jnp.asarray(swap),
         jnp.asarray(swap_table(angles, TILE)),
-        jnp.asarray(dft_table(theta, parts, group)),
+        jnp.asarray(table),
     )
     modes = modes.reshape(2, per_set, padded, full)
     shape = jax.ShapeDtypeStruct((per_set, 2, width, full), jnp.float32)

time: 54.4 us -> 55.6 us (1.022); the launches traced: 54.3 us -> 54.9 us
  Pallas kernels: 50.7 us -> 51.3 us
    pallas_call x1, Pallas kernels: 45.9 us -> 46.6 us  [body(): pl.pallas_call(functools.partial(exchange_kernel, parts, blocks, unit, gr...]
where the time goes in v2:
time: 55.6 us; the launch traced here: 54.9 us
  Pallas kernels  51.3 us (92%)
  local copies, waits for them, and re-layouts  2.89 us (5%)
  between operations  0.65 us (1%)
    pallas_call x1, Pallas kernels, body(): pl.pallas_call(functools.partial(exchange_kernel, parts, blocks, unit, gr...  46.6 us
    pallas_call x1, Pallas kernels, body(): pl.pallas_call(functools.partial(gram_kernel, rows ** (-0.5), width), gri...  4.78 us
    unnamed x6, local copies, waits for them, and re-layouts  2.89 us

profile of v2, /device:TPU:0, one launch (start us, length us, event | category | flops | bytes accessed | tf_op | source)
XLA Modules:
  0.0 54.9 jit_solution(2212389013808385475)
XLA Ops:
  0.6 0.0 copy-start
  0.6 1.1 %copy-done = bf16[16,160,128]{2,1,0:T(8,128)(2,1)S(1)} copy-done((bf16[16,160,128]{2,1,0:T(8,128)(2,1)S(1)}, bf16[16,160,128]{2,1,0:T(8,128)(2,1)}, u32[]{:S(2)}) %copy-start) | copy-done | bytes 655384
  1.7 0.0 copy-start.1
  1.7 0.9 %copy-done.1 = bf16[256,256]{1,0:T(8,128)(2,1)S(1)} copy-done((bf16[256,256]{1,0:T(8,128)(2,1)S(1)}, bf16[256,256]{1,0:T(8,128)(2,1)}, u32[]{:S(2)}) %copy-start.1) | copy-done | bytes 131096
  2.6 0.0 copy-start.2
  2.6 0.9 %copy-done.2 = bf16[256,256]{1,0:T(8,128)(2,1)S(1)} copy-done((bf16[256,256]{1,0:T(8,128)(2,1)S(1)}, bf16[256,256]{1,0:T(8,128)(2,1)}, u32[]{:S(2)}) %copy-start.2) | copy-done | bytes 131096
  3.5 46.6 %exchange.1 = bf16[16,160,256]{2,1,0:T(8,128)(2,1)S(1)} custom-call(bf16[16,160,128]{2,1,0:T(8,128)(2,1)S(1)} %copy-done, bf16[256,256]{1,0:T(8,128)(2,1)S(1)} %copy-done.1, bf16[256,256]{1,0:T(8,128)(2,1)S(1)} %copy-done.1, bf16[256,256]{1,0:T(8,128)(2,1)S(1)} %copy-done.2), custom_call_target="tpu_custom_call" | custom-call | tf_op jit(solution)/shard_map/exchange/pallas_call | solution.py:278
  50.1 4.8 %grams.1 = (f32[8,2,128,256]{3,2,1,0:T(8,128)}, f32[8,2,128,256]{3,2,1,0:T(8,128)}) custom-call(bf16[2,8,160,256]{3,2,1,0:T(8,128)(2,1)S(1)} %bitcast.1), custom_call_target="tpu_custom_call" | custom-call | tf_op jit(solution)/shard_map/grams/pallas_call | solution.py:310
Async XLA Ops:
  0.6 1.1 %copy-start = (bf16[16,160,128]{2,1,0:T(8,128)(2,1)S(1)}, bf16[16,160,128]{2,1,0:T(8,128)(2,1)}, u32[]{:S(2)}) copy-start(bf16[16,160,128]{2,1,0:T(8,128)(2,1)} %x_hbm.1) | copy-start | bytes 1966084
  1.7 0.9 %copy-start.1 = (bf16[256,256]{1,0:T(8,128)(2,1)S(1)}, bf16[256,256]{1,0:T(8,128)(2,1)}, u32[]{:S(2)}) copy-start(bf16[256,256]{1,0:T(8,128)(2,1)} %constant.4.clone.swap_in_hbm.swap_out_hbm) | copy-start | bytes 393220
  2.6 0.9 %copy-start.2 = (bf16[256,256]{1,0:T(8,128)(2,1)S(1)}, bf16[256,256]{1,0:T(8,128)(2,1)}, u32[]{:S(2)}) copy-start(bf16[256,256]{1,0:T(8,128)(2,1)} %constant.5.clone.table_hbm) | copy-start | bytes 393220

commit v3 on v2

--- a/solution.py
+++ b/solution.py
@@ -2,7 +2,6 @@
 
 import jax
 import jax.numpy as jnp
-import ml_dtypes
 import numpy as np
 from jax import lax
 from jax.experimental import pallas as pl
@@ -15,25 +14,29 @@
 
 def dft_table(theta, parts, group):
     angles = theta // parts
-    per_set = theta // 2 // parts
-    column = np.arange(theta)
-    owner, within = column // (2 * per_set), column % (2 * per_set)
-    wave = owner * per_set + within % per_set
-    index = (wave[:, None] * np.arange(theta)[None, :]) % theta
-    phase = index.astype(np.float32) * np.float32(2.0 * np.pi / theta)
-    scale = np.float32(theta ** -0.5)
-    imag = (within // per_set == 1)[:, None]
-    values = np.where(imag, -np.sin(phase), np.cos(phase)) * scale
-    values = values.reshape(parts, 1, 2 * per_set, parts, 1, angles)
-    eye = np.eye(group, dtype=np.float32).reshape(1, group, 1, 1, group, 1)
+    per_set = angles // 2
     side = theta * group
-    return (values * eye).reshape(side, side).astype(ml_dtypes.bfloat16)
+    row = lax.broadcasted_iota(jnp.int32, (side, side), 0)
+    column = lax.broadcasted_iota(jnp.int32, (side, side), 1)
+    unit = angles * group
+    within = row & (angles - 1)
+    imag = (within >= per_set).astype(jnp.int32)
+    wave = (row // unit) * per_set + (within & (per_set - 1))
+    angle = (column // unit) * angles + (column & (angles - 1))
+    index = (wave * angle + imag * (theta // 4)) & (theta - 1)
+    index = jnp.where(index >= theta // 2, index - theta, index)
+    values = jnp.cos(index.astype(jnp.float32) * (2.0 * np.pi / theta)) * theta ** -0.5
+    if group > 1:
+        same = (row & (unit - 1)) // angles == (column & (unit - 1)) // angles
+        values = jnp.where(same, values, 0.0)
+    return values.astype(jnp.bfloat16)
 
 
 def swap_table(outer, inner):
-    row = np.arange(outer * inner)
-    source = (row % inner) * outer + row // inner
-    return (source[:, None] == row[None, :]).astype(ml_dtypes.bfloat16)
+    row = lax.broadcasted_iota(jnp.int32, (outer * inner, outer * inner), 0)
+    column = lax.broadcasted_iota(jnp.int32, (outer * inner, outer * inner), 1)
+    hit = (row & (inner - 1)) * outer + row // inner == column
+    return jnp.where(hit, 1.0, 0.0).astype(jnp.bfloat16)
 
 
 def matmul(a, b):
@@ -42,9 +45,9 @@
 
 def exchange_kernel(
     parts, blocks, unit, groups, chunks,
-    x_hbm, swap_in_hbm, swap_out_hbm, table_hbm, modes_ref,
-    x_ref, swap_in, swap_out, table, pack, rx1, tx, rx2,
-    load, send1, recv1, send2, recv2, send3, recv3,
+    x_ref, modes_ref,
+    swap_in, swap_out, table, pack, rx1, tx, rx2,
+    send1, recv1, send2, recv2, send3, recv3,
 ):
     me = lax.axis_index("azim")
     tm = lax.axis_index("tm")
@@ -54,15 +57,6 @@
     per_chunk = groups // chunks
     padded = parts * blk // angles
 
-    loads = [
-        pltpu.make_async_copy(src, dst, load.at[i])
-        for i, (src, dst) in enumerate(
-            ((swap_in_hbm, swap_in), (x_hbm, x_ref), (table_hbm, table), (swap_out_hbm, swap_out))
-        )
-    ]
-    for copy in loads:
-        copy.start()
-
     barrier = pltpu.get_barrier_semaphore()
 
     def peer(s):
@@ -83,8 +77,7 @@
             barrier, inc=1, device_id=(lax.rem(tm + d, blocks), me), device_id_type=MESH
         )
 
-    loads[0].wait()
-    loads[1].wait()
+    swap_in[...] = swap_table(TILE, angles)
     step = TILE * angles
     for k in range(padded // TILE):
         if k * TILE < rows:
@@ -95,9 +88,11 @@
 
     pl.semaphore_wait(barrier, parts - 1 + blocks - 1)
 
+    parity = lax.rem(me, 2)
+    half = parts // 2
+
     def shift(i):
-        odd = lax.rem(i, 2)
-        return i // 2 + odd + (parts // 2) * (1 - odd)
+        return 1 + lax.rem((1 - parity) * (half - 1) + i, parts - 1)
 
     def copy1(c, s):
         to = peer(s)
@@ -178,8 +173,8 @@
     for c in range(chunks):
         loop(lambda s, c=c: copy1(c, s).start())
         rx1[c, me] = pack[pl.ds(pl.multiple_of(me * blk + c * cb, TILE), cb), :]
-    loads[2].wait()
-    loads[3].wait()
+    swap_out[...] = swap_table(angles, TILE)
+    table[...] = dft_table(angles * parts, parts, unit // angles)
 
     for c in range(chunks):
         loop(lambda s, c=c: landed1(c, s).wait_recv())
@@ -204,7 +199,21 @@
         def pass_on(s, c=c):
             landed2(c, s).wait_recv()
             forward(c, peer(s))
-        loop(pass_on)
+
+        for late in range(2):
+            flag = parity if late == 0 else 1 - parity
+
+            def far(j, carry, flag=flag):
+                pass_on(half + 2 * j + flag)
+                return carry
+
+            def near(j, carry, flag=flag):
+                s = 2 * j + 1 - flag
+                pl.when(s > 0)(lambda: pass_on(s))
+                return carry
+
+            lax.fori_loop(0, half // 2, near, 0)
+            lax.fori_loop(0, half // 2, far, 0)
         regroup(tm, c)
 
     for d in range(1, blocks):
@@ -271,25 +280,21 @@
     chunks = 2 if groups % 2 == 0 and padded % (2 * TILE) == 0 else 1
     full = blocks * width
 
-    swap = swap_table(TILE, angles)
-    table = dft_table(theta, parts, group)
     vmem = pl.BlockSpec(memory_space=pltpu.VMEM)
     dma = pltpu.SemaphoreType.DMA
     modes = pl.pallas_call(
         functools.partial(exchange_kernel, parts, blocks, unit, groups, chunks),
         out_shape=jax.ShapeDtypeStruct((angles, padded, full), jnp.bfloat16),
-        in_specs=[pl.BlockSpec(memory_space=pltpu.HBM)] * 4,
+        in_specs=[vmem],
         out_specs=vmem,
         scratch_shapes=[
-            pltpu.VMEM(pressure.shape, jnp.bfloat16),
-            pltpu.VMEM(swap.shape, jnp.bfloat16),
-            pltpu.VMEM(swap.shape, jnp.bfloat16),
-            pltpu.VMEM(table.shape, jnp.bfloat16),
+            pltpu.VMEM((TILE * angles, TILE * angles), jnp.bfloat16),
+            pltpu.VMEM((TILE * angles, TILE * angles), jnp.bfloat16),
+            pltpu.VMEM((theta * group, theta * group), jnp.bfloat16),
             pltpu.VMEM((parts * blk, width), jnp.bfloat16),
             pltpu.VMEM((chunks, parts, blk // chunks, width), jnp.bfloat16),
             pltpu.VMEM((chunks, parts, blk // chunks, width), jnp.bfloat16),
             pltpu.VMEM((blocks, chunks, parts, blk // chunks, width), jnp.bfloat16),
-            dma((4,)),
             dma((chunks, parts)), dma((chunks, parts)),
             dma((chunks, parts)), dma((chunks, parts)),
             dma((blocks, chunks, parts)), dma((blocks, chunks, parts)),
@@ -298,12 +303,7 @@
             collective_id=0, has_side_effects=True, vmem_limit_bytes=48 * 2**20
         ),
         name="exchange",
-    )(
-        pressure,
-        jnp.asarray(swap),
-        jnp.asarray(swap_table(angles, TILE)),
-        jnp.asarray(table),
-    )
+    )(pressure)
     modes = modes.reshape(2, per_set, padded, full)
     shape = jax.ShapeDtypeStruct((per_set, 2, width, full), jnp.float32)
     out = pl.BlockSpec((1, 2, width, full), lambda i: (i, 0, 0, 0))

time: 55.6 us -> 53.7 us (0.966)
  local copies, waits for them, and re-layouts: 2.89 us -> 1.08 us
    unnamed x6 -> x2, local copies, waits for them, and re-layouts: 2.89 us -> 1.08 us
where the time goes in v3:
time: 53.7 us; the launch traced here: 53 us
  Pallas kernels  51.3 us (96%)
  local copies, waits for them, and re-layouts  1.08 us (2%)
  between operations  0.65 us (1%)
    pallas_call x1, Pallas kernels, body(): pl.pallas_call(functools.partial(exchange_kernel, parts, blocks, unit, gr...  46.5 us
    pallas_call x1, Pallas kernels, body(): pl.pallas_call(functools.partial(gram_kernel, rows ** (-0.5), width), gri...  4.78 us
    unnamed x2, local copies, waits for them, and re-layouts  1.08 us

profile of v3, /device:TPU:0, one launch (start us, length us, event | category | flops | bytes accessed | tf_op | source)
XLA Modules:
  0.0 53.0 jit_solution(7414006450609817021)
XLA Ops:
  0.6 0.0 copy-start
  0.6 1.1 %copy-done = bf16[16,160,128]{2,1,0:T(8,128)(2,1)S(1)} copy-done((bf16[16,160,128]{2,1,0:T(8,128)(2,1)S(1)}, bf16[16,160,128]{2,1,0:T(8,128)(2,1)}, u32[]{:S(2)}) %copy-start) | copy-done | bytes 655384
  1.7 46.5 %exchange.1 = bf16[16,160,256]{2,1,0:T(8,128)(2,1)S(1)} custom-call(bf16[16,160,128]{2,1,0:T(8,128)(2,1)S(1)} %copy-done), custom_call_target="tpu_custom_call" | custom-call | tf_op jit(solution)/shard_map/exchange/pallas_call | solution.py:285
  48.2 4.8 %grams.1 = (f32[8,2,128,256]{3,2,1,0:T(8,128)}, f32[8,2,128,256]{3,2,1,0:T(8,128)}) custom-call(bf16[2,8,160,256]{3,2,1,0:T(8,128)(2,1)S(1)} %bitcast.1), custom_call_target="tpu_custom_call" | custom-call | tf_op jit(solution)/shard_map/grams/pallas_call | solution.py:310
Async XLA Ops:
  0.6 1.1 %copy-start = (bf16[16,160,128]{2,1,0:T(8,128)(2,1)S(1)}, bf16[16,160,128]{2,1,0:T(8,128)(2,1)}, u32[]{:S(2)}) copy-start(bf16[16,160,128]{2,1,0:T(8,128)(2,1)} %x_ref.1) | copy-start | bytes 1966084

commit v4 on v3

--- a/solution.py
+++ b/solution.py
@@ -277,7 +277,7 @@
         groups += 1
     blk = unit * groups
     padded = parts * groups * group
-    chunks = 2 if groups % 2 == 0 and padded % (2 * TILE) == 0 else 1
+    chunks = 1
     full = blocks * width
 
     vmem = pl.BlockSpec(memory_space=pltpu.VMEM)

time: 53.7 us -> 54.7 us (1.019)
  Pallas kernels: 51.3 us -> 52.7 us
    pallas_call x1, Pallas kernels: 46.5 us -> 47.9 us  [body(): pl.pallas_call(functools.partial(exchange_kernel, parts, blocks, unit, gr...]
where the time goes in v4:
time: 54.7 us; the launch traced here: 54.4 us
  Pallas kernels  52.7 us (96%)
  local copies, waits for them, and re-layouts  1.08 us (2%)
  between operations  0.65 us (1%)
    pallas_call x1, Pallas kernels, body(): pl.pallas_call(functools.partial(exchange_kernel, parts, blocks, unit, gr...  47.9 us
    pallas_call x1, Pallas kernels, body(): pl.pallas_call(functools.partial(gram_kernel, rows ** (-0.5), width), gri...  4.78 us

profile of v4, /device:TPU:0, one launch (start us, length us, event | category | flops | bytes accessed | tf_op | source)
XLA Modules:
  0.0 54.4 jit_solution(734045822636589738)
XLA Ops:
  0.6 0.0 copy-start
  0.6 1.1 %copy-done = bf16[16,160,128]{2,1,0:T(8,128)(2,1)S(1)} copy-done((bf16[16,160,128]{2,1,0:T(8,128)(2,1)S(1)}, bf16[16,160,128]{2,1,0:T(8,128)(2,1)}, u32[]{:S(2)}) %copy-start) | copy-done | bytes 655384
  1.7 47.9 %exchange.1 = bf16[16,160,256]{2,1,0:T(8,128)(2,1)S(1)} custom-call(bf16[16,160,128]{2,1,0:T(8,128)(2,1)S(1)} %copy-done), custom_call_target="tpu_custom_call" | custom-call | tf_op jit(solution)/shard_map/exchange/pallas_call | solution.py:285
  49.6 4.8 %grams.1 = (f32[8,2,128,256]{3,2,1,0:T(8,128)}, f32[8,2,128,256]{3,2,1,0:T(8,128)}) custom-call(bf16[2,8,160,256]{3,2,1,0:T(8,128)(2,1)S(1)} %bitcast.1), custom_call_target="tpu_custom_call" | custom-call | tf_op jit(solution)/shard_map/grams/pallas_call | solution.py:310
Async XLA Ops:
  0.6 1.1 %copy-start = (bf16[16,160,128]{2,1,0:T(8,128)(2,1)S(1)}, bf16[16,160,128]{2,1,0:T(8,128)(2,1)}, u32[]{:S(2)}) copy-start(bf16[16,160,128]{2,1,0:T(8,128)(2,1)} %x_ref.1) | copy-start | bytes 1966084

commit v5 on v4

v5 whole, which is shorter than its diff:
```python
import functools

import jax
import jax.numpy as jnp
import numpy as np
from jax import lax
from jax.experimental import pallas as pl
from jax.experimental.pallas import tpu as pltpu
from jax.sharding import PartitionSpec as P

MESH = pl.DeviceIdType.MESH
TILE = 16


def dft_table(theta, parts, group):
    angles = theta // parts
    per_set = angles // 2
    side = theta * group
    row = lax.broadcasted_iota(jnp.int32, (side, side), 0)
    column = lax.broadcasted_iota(jnp.int32, (side, side), 1)
    unit = angles * group
    within = row & (angles - 1)
    imag = (within >= per_set).astype(jnp.int32)
    wave = (row // unit) * per_set + (within & (per_set - 1))
    angle = (column // unit) * angles + (column & (angles - 1))
    index = (wave * angle + imag * (theta // 4)) & (theta - 1)
    index = jnp.where(index >= theta // 2, index - theta, index)
    values = jnp.cos(index.astype(jnp.float32) * (2.0 * np.pi / theta)) * theta ** -0.5
    if group > 1:
        same = (row & (unit - 1)) // angles == (column & (unit - 1)) // angles
        values = jnp.where(same, values, 0.0)
    return values.astype(jnp.bfloat16)


def swap_table(outer, inner):
    row = lax.broadcasted_iota(jnp.int32, (outer * inner, outer * inner), 0)
    column = lax.broadcasted_iota(jnp.int32, (outer * inner, outer * inner), 1)
    hit = (row & (inner - 1)) * outer + row // inner == column
    return jnp.where(hit, 1.0, 0.0).astype(jnp.bfloat16)


def matmul(a, pieces):
    width = pieces[0].shape[1]
    out = jnp.dot(a, jnp.concatenate(pieces, axis=1), preferred_element_type=jnp.float32)
    out = out.astype(jnp.bfloat16)
    return [out[:, i * width:(i + 1) * width] for i in range(len(pieces))]


def pairs(count):
    return [range(k, min(k + 2, count)) for k in range(0, count, 2)]


def partial_gram(left, real, imag):
    return [
        lax.dot_general(
            left, jnp.concatenate(right, axis=0), (((0,), (0,)), ((), ())),
            preferred_element_type=jnp.float32,
        )
        for right in ([real, imag], [imag, -real])
    ]


def exchange_kernel(parts, blocks, unit, groups, chunks, early, x_ref, *refs):
    if early:
        acc_ref, modes_ref, front, *refs = refs
    else:
        modes_ref, *refs = refs
    (swap_in, swap_out, table, pack, rx1, tx, rx2,
     send1, recv1, send2, recv2, send3, recv3) = refs
    me = lax.axis_index("azim")
    tm = lax.axis_index("tm")
    angles, rows, width = x_ref.shape
    blk = unit * groups
    cb = blk // chunks
    per_chunk = groups // chunks
    padded = parts * blk // angles

    barrier = pltpu.get_barrier_semaphore()

    def target(s):
        return lax.rem(me + s, parts)

    def origin(s):
        return lax.rem(me + parts - s, parts)

    def greet(s, carry):
        pl.semaphore_signal(barrier, inc=1, device_id=(tm, target(s)), device_id_type=MESH)
        return carry

    lax.fori_loop(1, parts, greet, 0)
    for d in range(1, blocks):
        pl.semaphore_signal(
            barrier, inc=1, device_id=(lax.rem(tm + d, blocks), me), device_id_type=MESH
        )

    swap_in[...] = swap_table(TILE, angles)
    step = TILE * angles
    whole = rows // TILE
    for pair in pairs(whole):
        given = [x_ref[:, k * TILE:(k + 1) * TILE, :].reshape(step, width) for k in pair]
        for k, out in zip(pair, matmul(swap_in[...], given)):
            pack[k * step:(k + 1) * step, :] = out
    for k in range(whole, padded // TILE):
        pack[k * step:(k + 1) * step, :] = jnp.zeros((step, width), jnp.bfloat16)

    pl.semaphore_wait(barrier, parts - 1 + blocks - 1)

    def shift(i):
        return 1 + lax.rem(parts // 2 - 1 + i, parts - 1)

    def copy1(c, s):
        to = target(s)
        return pltpu.make_async_remote_copy(
            src_ref=pack.at[pl.ds(pl.multiple_of(to * blk + c * cb, TILE), cb), :],
            dst_ref=rx1.at[c, me],
            send_sem=send1.at[c, s],
            recv_sem=recv1.at[c, s],
            device_id=(tm, to),
            device_id_type=MESH,
        )

    def copy2(c, s):
        to = target(s)
        return pltpu.make_async_remote_copy(
            src_ref=tx.at[c, to],
            dst_ref=rx2.at[tm, c, me],
            send_sem=send2.at[c, s],
            recv_sem=recv2.at[c, s],
            device_id=(tm, to),
            device_id_type=MESH,
        )

    def landed1(c, s):
        source = origin(s)
        here = rx1.at[c, source]
        return pltpu.make_async_remote_copy(
            src_ref=here, dst_ref=here, send_sem=send1.at[c, s], recv_sem=recv1.at[c, s],
            device_id=(tm, source), device_id_type=MESH,
        )

    def landed2(c, s):
        source = origin(s)
        here = rx2.at[tm, c, source]
        return pltpu.make_async_remote_copy(
            src_ref=here, dst_ref=here, send_sem=send2.at[c, s], recv_sem=recv2.at[c, s],
            device_id=(tm, source), device_id_type=MESH,
        )

    def copy3(c, source, d):
        here = rx2.at[tm, c, source]
        return pltpu.make_async_remote_copy(
            src_ref=here, dst_ref=here,
            send_sem=send3.at[d - 1, c, source], recv_sem=recv3.at[d - 1, c, source],
            device_id=(lax.rem(tm + d, blocks), me), device_id_type=MESH,
        )

    def landed3(c, source, d):
        here = rx2.at[lax.rem(tm + blocks - d, blocks), c, source]
        return pltpu.make_async_remote_copy(
            src_ref=here, dst_ref=here,
            send_sem=send3.at[d - 1, c, source], recv_sem=recv3.at[d - 1, c, source],
            device_id=(lax.rem(tm + blocks - d, blocks), me), device_id_type=MESH,
        )

    def guarded(condition, act):
        if blocks == 2:
            act()
        else:
            pl.when(condition)(act)

    def needed_by(d):
        return lax.rem(tm + d, blocks) >= tm - 1

    def needed_from(d):
        return lax.rem(tm + blocks - d, blocks) <= tm + 1

    def loop(body, first=0, last=parts - 1):
        def run(i, carry):
            body(shift(i))
            return carry
        lax.fori_loop(first, last, run, 0)

    def forward(c, source):
        for d in range(1, blocks):
            guarded(needed_by(d), lambda d=d: copy3(c, source, d).start())

    for c in range(chunks):
        loop(lambda s, c=c: copy1(c, s).start())
        rx1[c, me] = pack[pl.ds(pl.multiple_of(me * blk + c * cb, TILE), cb), :]
    swap_out[...] = swap_table(angles, TILE)
    table[...] = dft_table(angles * parts, parts, unit // angles)

    for c in range(chunks):
        loop(lambda s, c=c: landed1(c, s).wait_recv())
        for pair in pairs(per_chunk):
            fields = [
                rx1[c, :, q * unit:(q + 1) * unit, :].reshape(parts * unit, width) for q in pair
            ]
            for q, out in zip(pair, matmul(table[...], fields)):
                tx[c, :, q * unit:(q + 1) * unit, :] = out.reshape(parts, unit, width)
        loop(lambda s, c=c: copy2(c, s).start())
        rx2[tm, c, me] = tx[c, me]
        forward(c, me)

    span = padded // chunks

    per_set = angles // 2

    def place(block, c, k, value):
        lanes = pl.ds(pl.multiple_of(block * width, width), width)
        if c < early:
            start = c * span + k * TILE
            front[:, start:start + TILE, lanes] = value
        else:
            start = (c - early) * span + k * TILE
            modes_ref[:, start:start + TILE, lanes] = value

    def regroup(block, c):
        flat = rx2.at[block, c].reshape(parts * cb, width)
        for pair in pairs(span // TILE):
            given = [flat[k * step:(k + 1) * step, :] for k in pair]
            for k, out in zip(pair, matmul(swap_out[...], given)):
                place(block, c, k, out.reshape(angles, TILE, width))

    def take_others(c):
        for d in range(1, blocks):
            other = lax.rem(tm + blocks - d, blocks)

            def take(d=d, other=other):
                def arrive(i, carry):
                    landed3(c, i, d).wait_recv()
                    return carry
                lax.fori_loop(0, parts, arrive, 0)
                regroup(other, c)

            guarded(needed_from(d), take)
            if blocks > 2:
                @pl.when(jnp.logical_not(needed_from(d)))
                def _(other=other):
                    for k in range(span // TILE):
                        place(other, c, k, jnp.zeros((angles, TILE, width), jnp.bfloat16))

    own = pl.ds(pl.multiple_of(tm * width, width), width)

    def early_gram(m):
        left = jnp.concatenate([front[m, :, own], front[per_set + m, :, own]], axis=0)
        for p, out in enumerate(partial_gram(left, front[m], front[per_set + m])):
            acc_ref[m, p] = out

    for c in range(chunks):
        def pass_on(s, c=c):
            landed2(c, s).wait_recv()
            forward(c, origin(s))

        if early and c == chunks - 1:
            for m in range(per_set):
                early_gram(m)
                loop(pass_on, (parts - 1) * m // per_set, (parts - 1) * (m + 1) // per_set)
        else:
            loop(pass_on)
        regroup(tm, c)
        if c > 0:
            take_others(c - 1)
    take_others(chunks - 1)

    for c in range(chunks):
        loop(lambda s, c=c: copy1(c, s).wait_send())
        loop(lambda s, c=c: copy2(c, s).wait_send())
        for d in range(1, blocks):
            def sent(d=d, c=c):
                def one(i, carry):
                    copy3(c, i, d).wait_send()
                    return carry
                lax.fori_loop(0, parts, one, 0)
            guarded(needed_by(d), sent)


def gram_kernel(gain, width, has_acc, *refs):
    if has_acc:
        acc_ref, modes_ref, xx_hbm, xy_hbm, xx, xy, sem = refs
    else:
        modes_ref, xx_hbm, xy_hbm, xx, xy, sem = refs
    tm = lax.axis_index("tm")
    count, full = modes_ref.shape[0] // 2, modes_ref.shape[2]
    limit = (tm + 1) * width
    columns = lax.broadcasted_iota(jnp.int32, (width, full), 1)
    keep_xx = columns < limit
    keep_xy = columns < jnp.minimum(limit, full - 1)
    own = pl.ds(pl.multiple_of(tm * width, width), width)
    copies = []
    for m in range(count):
        left = jnp.concatenate([modes_ref[m, :, own], modes_ref[count + m, :, own]], axis=0)
        for p, product in enumerate(partial_gram(left, modes_ref[m], modes_ref[count + m])):
            if has_acc:
                product = product + acc_ref[m, p]
            product = product * gain
            xx[m, p] = jnp.where(keep_xx, product, 0.0)
            xy[m, p] = jnp.where(keep_xy, pltpu.roll(product, full - 1, 1), 0.0)
        for i, (src, dst) in enumerate(((xx, xx_hbm), (xy, xy_hbm))):
            copies.append(pltpu.make_async_copy(src.at[m], dst.at[m], sem.at[i, m]))
            copies[-1].start()
    for copy in copies:
        copy.wait()


def body(parts, blocks, pressure):
    angles, rows, width = pressure.shape
    theta = angles * parts
    per_set = theta // 2 // parts
    group = max(1, TILE // angles)
    unit = group * angles
    groups = -(-rows // (parts * group))
    while parts * groups * group % TILE:
        groups += 1
    blk = unit * groups
    padded = parts * groups * group
    chunks = max(
        c for c in range(1, 6) if groups % c == 0 and padded % (c * TILE) == 0
    )
    early = max(chunks - 2, 0)
    span = padded // chunks
    full = blocks * width

    vmem = pl.BlockSpec(memory_space=pltpu.VMEM)
    dma = pltpu.SemaphoreType.DMA
    modes_shape = jax.ShapeDtypeStruct((angles, (chunks - early) * span, full), jnp.bfloat16)
    gram_shape = jax.ShapeDtypeStruct((per_set, 2, width, full), jnp.float32)
    front = [pltpu.VMEM((angles, early * span, full), jnp.bfloat16)] if early else []
    made = pl.pallas_call(
        functools.partial(exchange_kernel, parts, blocks, unit, groups, chunks, early),
        out_shape=(gram_shape, modes_shape) if early else (modes_shape,),
        in_specs=[vmem],
        out_specs=(vmem, vmem) if early else (vmem,),
        scratch_shapes=front + [
            pltpu.VMEM((TILE * angles, TILE * angles), jnp.bfloat16),
            pltpu.VMEM((TILE * angles, TILE * angles), jnp.bfloat16),
            pltpu.VMEM((theta * group, theta * group), jnp.bfloat16),
            pltpu.VMEM((parts * blk, width), jnp.bfloat16),
            pltpu.VMEM((chunks, parts, blk // chunks, width), jnp.bfloat16),
            pltpu.VMEM((chunks, parts, blk // chunks, width), jnp.bfloat16),
            pltpu.VMEM((blocks, chunks, parts, blk // chunks, width), jnp.bfloat16),
            dma((chunks, parts)), dma((chunks, parts)),
            dma((chunks, parts)), dma((chunks, parts)),
            dma((blocks - 1, chunks, parts)), dma((blocks - 1, chunks, parts)),
        ],
        compiler_params=pltpu.CompilerParams(
            collective_id=0, has_side_effects=True, vmem_limit_bytes=48 * 2**20
        ),
        name="exchange",
    )(pressure)
    return pl.pallas_call(
        functools.partial(gram_kernel, rows ** -0.5, width, early > 0),
        out_shape=(gram_shape, gram_shape),
        in_specs=[vmem] * len(made),
        out_specs=(pl.BlockSpec(memory_space=pl.ANY),) * 2,
        scratch_shapes=[
            pltpu.VMEM(gram_shape.shape, jnp.float32),
            pltpu.VMEM(gram_shape.shape, jnp.float32),
            dma((2, per_set)),
        ],
        compiler_params=pltpu.CompilerParams(vmem_limit_bytes=48 * 2**20),
        name="grams",
    )(*made)


def solution(mesh):
    parts, blocks = mesh.shape["azim"], mesh.shape["tm"]
    in_specs = (P("azim", None, "tm"),)
    out_specs = (P("azim", None, "tm", None), P("azim", None, "tm", None))
    return jax.shard_map(
        functools.partial(body, parts, blocks),
        mesh=mesh, in_specs=in_specs, out_specs=out_specs, check_vma=False,
    )
```

time: 54.7 us -> 53.9 us (0.985)
  Pallas kernels: 52.7 us -> 52 us
    pallas_call x1, Pallas kernels: 4.78 us -> 2.46 us  [body(): pl.pallas_call(functools.partial(gram_kernel, rows ** (-0.5), width, earl...]
    pallas_call x1, Pallas kernels: 47.9 us -> 49.5 us  [body(): pl.pallas_call(functools.partial(exchange_kernel, parts, blocks, unit, gr...]
where the time goes in v5:
time: 53.9 us; the launch traced here: 53.7 us
  Pallas kernels  52 us (96%)
  local copies, waits for them, and re-layouts  1.08 us (2%)
  between operations  0.65 us (1%)
    pallas_call x1, Pallas kernels, body(): pl.pallas_call(functools.partial(exchange_kernel, parts, blocks, unit, gr...  49.5 us
    pallas_call x1, Pallas kernels, body(): pl.pallas_call(functools.partial(gram_kernel, rows ** (-0.5), width, earl...  2.46 us
    unnamed x2, local copies, waits for them, and re-layouts  1.08 us

profile of v5, /device:TPU:0, one launch (start us, length us, event | category | flops | bytes accessed | tf_op | source)
XLA Modules:
  0.0 53.7 jit_solution(17488657261698765150)
XLA Ops:
  0.6 0.0 copy-start
  0.6 1.1 %copy-done = bf16[16,160,128]{2,1,0:T(8,128)(2,1)S(1)} copy-done((bf16[16,160,128]{2,1,0:T(8,128)(2,1)S(1)}, bf16[16,160,128]{2,1,0:T(8,128)(2,1)}, u32[]{:S(2)}) %copy-start) | copy-done | bytes 655384
  1.7 49.5 %exchange.1 = (f32[8,2,128,256]{3,2,1,0:T(8,128)S(1)}, bf16[16,64,256]{2,1,0:T(8,128)(2,1)S(1)}) custom-call(bf16[16,160,128]{2,1,0:T(8,128)(2,1)S(1)} %copy-done), custom_call_target="tpu_custom_call" | custom-call | tf_op jit(solution)/shard_map/exchange/pallas_call | solution.py:329
  51.3 2.5 %grams.1 = (f32[8,2,128,256]{3,2,1,0:T(8,128)}, f32[8,2,128,256]{3,2,1,0:T(8,128)}) custom-call(f32[8,2,128,256]{3,2,1,0:T(8,128)S(1)} %get-tuple-element.4.refs_0_, bf16[16,64,256]{2,1,0:T(8,128)(2,1)S(1)} %get-tuple-element.5.refs_1_), custom_call_target="tpu_custom_call" | custom-call | tf_op jit(solution)/shard_map/grams/pallas_call | solution.py:351
Async XLA Ops:
  0.6 1.1 %copy-start = (bf16[16,160,128]{2,1,0:T(8,128)(2,1)S(1)}, bf16[16,160,128]{2,1,0:T(8,128)(2,1)}, u32[]{:S(2)}) copy-start(bf16[16,160,128]{2,1,0:T(8,128)(2,1)} %x_ref.1) | copy-start | bytes 1966084

commit v6 on v5

--- a/solution.py
+++ b/solution.py
@@ -253,15 +253,19 @@
             forward(c, origin(s))
 
         if early and c == chunks - 1:
+            head = parts // 4
+            loop(pass_on, 0, head)
+            for e in range(early):
+                take_others(e)
+            rest = parts - 1 - head
             for m in range(per_set):
                 early_gram(m)
-                loop(pass_on, (parts - 1) * m // per_set, (parts - 1) * (m + 1) // per_set)
+                loop(pass_on, head + rest * m // per_set, head + rest * (m + 1) // per_set)
         else:
             loop(pass_on)
         regroup(tm, c)
-        if c > 0:
-            take_others(c - 1)
-    take_others(chunks - 1)
+    for c in range(early, chunks):
+        take_others(c)
 
     for c in range(chunks):
         loop(lambda s, c=c: copy1(c, s).wait_send())
@@ -315,9 +319,9 @@
     blk = unit * groups
     padded = parts * groups * group
     chunks = max(
-        c for c in range(1, 6) if groups % c == 0 and padded % (c * TILE) == 0
+        c for c in (1, 2) if groups % c == 0 and padded % (c * TILE) == 0
     )
-    early = max(chunks - 2, 0)
+    early = chunks // 2
     span = padded // chunks
     full = blocks * width
 

time: 53.9 us -> 49.5 us (0.918)
  Pallas kernels: 52 us -> 47.6 us
    pallas_call x1, Pallas kernels: 49.5 us -> 45.1 us  [body(): pl.pallas_call(functools.partial(exchange_kernel, parts, blocks, unit, gr...]
where the time goes in v6:
time: 49.5 us; the launch traced here: 49.3 us
  Pallas kernels  47.6 us (96%)
  local copies, waits for them, and re-layouts  1.08 us (2%)
  between operations  0.65 us (1%)
    pallas_call x1, Pallas kernels, body(): pl.pallas_call(functools.partial(exchange_kernel, parts, blocks, unit, gr...  45.1 us
    pallas_call x1, Pallas kernels, body(): pl.pallas_call(functools.partial(gram_kernel, rows ** (-0.5), width, earl...  2.48 us
    unnamed x2, local copies, waits for them, and re-layouts  1.08 us

profile of v6, /device:TPU:0, one launch (start us, length us, event | category | flops | bytes accessed | tf_op | source)
XLA Modules:
  0.0 49.3 jit_solution(10163159545463259177)
XLA Ops:
  0.6 0.0 copy-start
  0.6 1.1 %copy-done = bf16[16,160,128]{2,1,0:T(8,128)(2,1)S(1)} copy-done((bf16[16,160,128]{2,1,0:T(8,128)(2,1)S(1)}, bf16[16,160,128]{2,1,0:T(8,128)(2,1)}, u32[]{:S(2)}) %copy-start) | copy-done | bytes 655384
  1.7 45.1 %exchange.1 = (f32[8,2,128,256]{3,2,1,0:T(8,128)S(1)}, bf16[16,80,256]{2,1,0:T(8,128)(2,1)S(1)}) custom-call(bf16[16,160,128]{2,1,0:T(8,128)(2,1)S(1)} %copy-done), custom_call_target="tpu_custom_call" | custom-call | tf_op jit(solution)/shard_map/exchange/pallas_call | solution.py:333
  46.8 2.5 %grams.1 = (f32[8,2,128,256]{3,2,1,0:T(8,128)}, f32[8,2,128,256]{3,2,1,0:T(8,128)}) custom-call(f32[8,2,128,256]{3,2,1,0:T(8,128)S(1)} %get-tuple-element.4.refs_0_, bf16[16,80,256]{2,1,0:T(8,128)(2,1)S(1)} %get-tuple-element.5.refs_1_), custom_call_target="tpu_custom_call" | custom-call | tf_op jit(solution)/shard_map/grams/pallas_call | solution.py:355
Async XLA Ops:
  0.6 1.1 %copy-start = (bf16[16,160,128]{2,1,0:T(8,128)(2,1)S(1)}, bf16[16,160,128]{2,1,0:T(8,128)(2,1)}, u32[]{:S(2)}) copy-start(bf16[16,160,128]{2,1,0:T(8,128)(2,1)} %x_ref.1) | copy-start | bytes 1966084

commit v7 on v6

--- a/solution.py
+++ b/solution.py
@@ -105,8 +105,11 @@
 
     pl.semaphore_wait(barrier, parts - 1 + blocks - 1)
 
+    def order(parity, i):
+        return 1 + lax.rem((1 - parity) * (parts // 2 - 1) + i, parts - 1)
+
     def shift(i):
-        return 1 + lax.rem(parts // 2 - 1 + i, parts - 1)
+        return order(lax.rem(me, 2), i)
 
     def copy1(c, s):
         to = target(s)
@@ -177,6 +180,14 @@
     def loop(body, first=0, last=parts - 1):
         def run(i, carry):
             body(shift(i))
+            return carry
+        lax.fori_loop(first, last, run, 0)
+
+    def arrivals(body, first=0, last=parts - 1):
+        def run(i, carry):
+            for parity in range(2):
+                s = order(parity, i)
+                pl.when(lax.rem(origin(s), 2) == parity)(functools.partial(body, s))
             return carry
         lax.fori_loop(first, last, run, 0)
 
@@ -254,15 +265,15 @@
 
         if early and c == chunks - 1:
             head = parts // 4
-            loop(pass_on, 0, head)
+            arrivals(pass_on, 0, head)
             for e in range(early):
                 take_others(e)
             rest = parts - 1 - head
             for m in range(per_set):
                 early_gram(m)
-                loop(pass_on, head + rest * m // per_set, head + rest * (m + 1) // per_set)
+                arrivals(pass_on, head + rest * m // per_set, head + rest * (m + 1) // per_set)
         else:
-            loop(pass_on)
+            arrivals(pass_on)
         regroup(tm, c)
     for c in range(early, chunks):
         take_others(c)

time: 49.5 us -> 49.8 us (level)
  no operation moved by 1% of the time
where the time goes in v7:
time: 49.8 us; the launch traced here: 49.6 us
  Pallas kernels  47.9 us (96%)
  local copies, waits for them, and re-layouts  1.08 us (2%)
  between operations  0.65 us (1%)
    pallas_call x1, Pallas kernels, body(): pl.pallas_call(functools.partial(exchange_kernel, parts, blocks, unit, gr...  45.4 us
    pallas_call x1, Pallas kernels, body(): pl.pallas_call(functools.partial(gram_kernel, rows ** (-0.5), width, earl...  2.46 us
    unnamed x2, local copies, waits for them, and re-layouts  1.08 us

profile of v7, /device:TPU:0, one launch (start us, length us, event | category | flops | bytes accessed | tf_op | source)
XLA Modules:
  0.0 49.6 jit_solution(16007812015374764867)
XLA Ops:
  0.6 0.0 copy-start
  0.6 1.1 %copy-done = bf16[16,160,128]{2,1,0:T(8,128)(2,1)S(1)} copy-done((bf16[16,160,128]{2,1,0:T(8,128)(2,1)S(1)}, bf16[16,160,128]{2,1,0:T(8,128)(2,1)}, u32[]{:S(2)}) %copy-start) | copy-done | bytes 655384
  1.7 45.4 %exchange.1 = (f32[8,2,128,256]{3,2,1,0:T(8,128)S(1)}, bf16[16,80,256]{2,1,0:T(8,128)(2,1)S(1)}) custom-call(bf16[16,160,128]{2,1,0:T(8,128)(2,1)S(1)} %copy-done), custom_call_target="tpu_custom_call" | custom-call | tf_op jit(solution)/shard_map/exchange/pallas_call | solution.py:344
  47.1 2.5 %grams.1 = (f32[8,2,128,256]{3,2,1,0:T(8,128)}, f32[8,2,128,256]{3,2,1,0:T(8,128)}) custom-call(f32[8,2,128,256]{3,2,1,0:T(8,128)S(1)} %get-tuple-element.4.refs_0_, bf16[16,80,256]{2,1,0:T(8,128)(2,1)S(1)} %get-tuple-element.5.refs_1_), custom_call_target="tpu_custom_call" | custom-call | tf_op jit(solution)/shard_map/grams/pallas_call | solution.py:366
Async XLA Ops:
  0.6 1.1 %copy-start = (bf16[16,160,128]{2,1,0:T(8,128)(2,1)S(1)}, bf16[16,160,128]{2,1,0:T(8,128)(2,1)}, u32[]{:S(2)}) copy-start(bf16[16,160,128]{2,1,0:T(8,128)(2,1)} %x_ref.1) | copy-start | bytes 1966084

commit v8 on v6

--- a/solution.py
+++ b/solution.py
@@ -198,12 +198,13 @@
             ]
             for q, out in zip(pair, matmul(table[...], fields)):
                 tx[c, :, q * unit:(q + 1) * unit, :] = out.reshape(parts, unit, width)
-        loop(lambda s, c=c: copy2(c, s).start())
+        if c == 0 or not early:
+            loop(lambda s, c=c: copy2(c, s).start())
         rx2[tm, c, me] = tx[c, me]
         forward(c, me)
 
     span = padded // chunks
-
+    window = min(6, parts - 1)
     per_set = angles // 2
 
     def place(block, c, k, value):
@@ -252,15 +253,30 @@
             landed2(c, s).wait_recv()
             forward(c, origin(s))
 
+        def pass_and_send(first, last, ahead, c=c):
+            def run(i, carry):
+                pass_on(shift(i))
+                copy2(chunks - 1, shift(i + ahead)).start()
+                return carry
+            lax.fori_loop(first, last, run, 0)
+
         if early and c == chunks - 1:
-            head = parts // 4
-            loop(pass_on, 0, head)
+            paced = parts - 1 - window
+            head = min(parts // 4, paced)
+            pass_and_send(0, head, window)
             for e in range(early):
                 take_others(e)
             rest = parts - 1 - head
             for m in range(per_set):
                 early_gram(m)
-                loop(pass_on, head + rest * m // per_set, head + rest * (m + 1) // per_set)
+                first, last = head + rest * m // per_set, head + rest * (m + 1) // per_set
+                if first < paced:
+                    pass_and_send(first, min(last, paced), window)
+                if last > paced:
+                    loop(pass_on, max(first, paced), last)
+        elif early and c == chunks - 2:
+            loop(pass_on, 0, parts - 1 - window)
+            pass_and_send(parts - 1 - window, parts - 1, window - parts + 1)
         else:
             loop(pass_on)
         regroup(tm, c)

time: 49.5 us -> 52 us (1.051)
  Pallas kernels: 47.6 us -> 50.2 us
    pallas_call x1, Pallas kernels: 45.1 us -> 47.7 us  [body(): pl.pallas_call(functools.partial(exchange_kernel, parts, blocks, unit, gr...]
where the time goes in v8:
time: 52 us; the launch traced here: 51.9 us
  Pallas kernels  50.2 us (97%)
  local copies, waits for them, and re-layouts  1.08 us (2%)
  between operations  0.65 us (1%)
    pallas_call x1, Pallas kernels, body(): pl.pallas_call(functools.partial(exchange_kernel, parts, blocks, unit, gr...  47.7 us
    pallas_call x1, Pallas kernels, body(): pl.pallas_call(functools.partial(gram_kernel, rows ** (-0.5), width, earl...  2.48 us
    unnamed x2, local copies, waits for them, and re-layouts  1.08 us

profile of v8, /device:TPU:0, one launch (start us, length us, event | category | flops | bytes accessed | tf_op | source)
XLA Modules:
  0.0 51.9 jit_solution(17430662029914328700)
XLA Ops:
  0.6 0.0 copy-start
  0.6 1.1 %copy-done = bf16[16,160,128]{2,1,0:T(8,128)(2,1)S(1)} copy-done((bf16[16,160,128]{2,1,0:T(8,128)(2,1)S(1)}, bf16[16,160,128]{2,1,0:T(8,128)(2,1)}, u32[]{:S(2)}) %copy-start) | copy-done | bytes 655384
  1.7 47.7 %exchange.1 = (f32[8,2,128,256]{3,2,1,0:T(8,128)S(1)}, bf16[16,80,256]{2,1,0:T(8,128)(2,1)S(1)}) custom-call(bf16[16,160,128]{2,1,0:T(8,128)(2,1)S(1)} %copy-done), custom_call_target="tpu_custom_call" | custom-call | tf_op jit(solution)/shard_map/exchange/pallas_call | solution.py:349
  49.4 2.5 %grams.1 = (f32[8,2,128,256]{3,2,1,0:T(8,128)}, f32[8,2,128,256]{3,2,1,0:T(8,128)}) custom-call(f32[8,2,128,256]{3,2,1,0:T(8,128)S(1)} %get-tuple-element.4.refs_0_, bf16[16,80,256]{2,1,0:T(8,128)(2,1)S(1)} %get-tuple-element.5.refs_1_), custom_call_target="tpu_custom_call" | custom-call | tf_op jit(solution)/shard_map/grams/pallas_call | solution.py:371
Async XLA Ops:
  0.6 1.1 %copy-start = (bf16[16,160,128]{2,1,0:T(8,128)(2,1)S(1)}, bf16[16,160,128]{2,1,0:T(8,128)(2,1)}, u32[]{:S(2)}) copy-start(bf16[16,160,128]{2,1,0:T(8,128)(2,1)} %x_ref.1) | copy-start | bytes 1966084

commit v9 on v6

--- a/solution.py
+++ b/solution.py
@@ -113,8 +113,8 @@
         return pltpu.make_async_remote_copy(
             src_ref=pack.at[pl.ds(pl.multiple_of(to * blk + c * cb, TILE), cb), :],
             dst_ref=rx1.at[c, me],
-            send_sem=send1.at[c, s],
-            recv_sem=recv1.at[c, s],
+            send_sem=send1.at[c],
+            recv_sem=recv1.at[c],
             device_id=(tm, to),
             device_id_type=MESH,
         )
@@ -124,25 +124,31 @@
         return pltpu.make_async_remote_copy(
             src_ref=tx.at[c, to],
             dst_ref=rx2.at[tm, c, me],
-            send_sem=send2.at[c, s],
+            send_sem=send2.at[c],
             recv_sem=recv2.at[c, s],
             device_id=(tm, to),
             device_id_type=MESH,
         )
 
-    def landed1(c, s):
-        source = origin(s)
-        here = rx1.at[c, source]
-        return pltpu.make_async_remote_copy(
-            src_ref=here, dst_ref=here, send_sem=send1.at[c, s], recv_sem=recv1.at[c, s],
-            device_id=(tm, source), device_id_type=MESH,
+    def all1(c):
+        there = rx1.at[c, pl.ds(0, parts - 1)]
+        return pltpu.make_async_remote_copy(
+            src_ref=there, dst_ref=there, send_sem=send1.at[c], recv_sem=recv1.at[c],
+            device_id=(tm, target(1)), device_id_type=MESH,
+        )
+
+    def all2(c):
+        there = tx.at[c, pl.ds(0, parts - 1)]
+        return pltpu.make_async_remote_copy(
+            src_ref=there, dst_ref=there, send_sem=send2.at[c], recv_sem=recv2.at[c, 0],
+            device_id=(tm, target(1)), device_id_type=MESH,
         )
 
     def landed2(c, s):
         source = origin(s)
         here = rx2.at[tm, c, source]
         return pltpu.make_async_remote_copy(
-            src_ref=here, dst_ref=here, send_sem=send2.at[c, s], recv_sem=recv2.at[c, s],
+            src_ref=here, dst_ref=here, send_sem=send2.at[c], recv_sem=recv2.at[c, s],
             device_id=(tm, source), device_id_type=MESH,
         )
 
@@ -150,16 +156,15 @@
         here = rx2.at[tm, c, source]
         return pltpu.make_async_remote_copy(
             src_ref=here, dst_ref=here,
-            send_sem=send3.at[d - 1, c, source], recv_sem=recv3.at[d - 1, c, source],
+            send_sem=send3.at[d - 1, c], recv_sem=recv3.at[d - 1, c],
             device_id=(lax.rem(tm + d, blocks), me), device_id_type=MESH,
         )
 
-    def landed3(c, source, d):
-        here = rx2.at[lax.rem(tm + blocks - d, blocks), c, source]
-        return pltpu.make_async_remote_copy(
-            src_ref=here, dst_ref=here,
-            send_sem=send3.at[d - 1, c, source], recv_sem=recv3.at[d - 1, c, source],
-            device_id=(lax.rem(tm + blocks - d, blocks), me), device_id_type=MESH,
+    def all3(c, d, block):
+        there = rx2.at[block, c]
+        return pltpu.make_async_remote_copy(
+            src_ref=there, dst_ref=there, send_sem=send3.at[d - 1, c], recv_sem=recv3.at[d - 1, c],
+            device_id=(lax.rem(tm + d, blocks), me), device_id_type=MESH,
         )
 
     def guarded(condition, act):
@@ -191,7 +196,7 @@
     table[...] = dft_table(angles * parts, parts, unit // angles)
 
     for c in range(chunks):
-        loop(lambda s, c=c: landed1(c, s).wait_recv())
+        all1(c).wait_recv()
         for pair in pairs(per_chunk):
             fields = [
                 rx1[c, :, q * unit:(q + 1) * unit, :].reshape(parts * unit, width) for q in pair
@@ -227,10 +232,7 @@
             other = lax.rem(tm + blocks - d, blocks)
 
             def take(d=d, other=other):
-                def arrive(i, carry):
-                    landed3(c, i, d).wait_recv()
-                    return carry
-                lax.fori_loop(0, parts, arrive, 0)
+                all3(c, d, other).wait_recv()
                 regroup(other, c)
 
             guarded(needed_from(d), take)
@@ -264,19 +266,14 @@
         else:
             loop(pass_on)
         regroup(tm, c)
+    for c in range(chunks):
+        all1(c).wait_send()
+        all2(c).wait_send()
     for c in range(early, chunks):
         take_others(c)
-
-    for c in range(chunks):
-        loop(lambda s, c=c: copy1(c, s).wait_send())
-        loop(lambda s, c=c: copy2(c, s).wait_send())
+    for c in range(chunks):
         for d in range(1, blocks):
-            def sent(d=d, c=c):
-                def one(i, carry):
-                    copy3(c, i, d).wait_send()
-                    return carry
-                lax.fori_loop(0, parts, one, 0)
-            guarded(needed_by(d), sent)
+            guarded(needed_by(d), lambda c=c, d=d: all3(c, d, tm).wait_send())
 
 
 def gram_kernel(gain, width, has_acc, *refs):
@@ -343,9 +340,9 @@
             pltpu.VMEM((chunks, parts, blk // chunks, width), jnp.bfloat16),
             pltpu.VMEM((chunks, parts, blk // chunks, width), jnp.bfloat16),
             pltpu.VMEM((blocks, chunks, parts, blk // chunks, width), jnp.bfloat16),
-            dma((chunks, parts)), dma((chunks, parts)),
-            dma((chunks, parts)), dma((chunks, parts)),
-            dma((blocks - 1, chunks, parts)), dma((blocks - 1, chunks, parts)),
+            dma((chunks,)), dma((chunks,)),
+            dma((chunks,)), dma((chunks, parts)),
+            dma((blocks - 1, chunks)), dma((blocks - 1, chunks)),
         ],
         compiler_params=pltpu.CompilerParams(
             collective_id=0, has_side_effects=True, vmem_limit_bytes=48 * 2**20

time: 49.5 us -> 47 us (0.949)
  Pallas kernels: 47.6 us -> 45.1 us
    pallas_call x1, Pallas kernels: 45.1 us -> 42.7 us  [body(): pl.pallas_call(functools.partial(exchange_kernel, parts, blocks, unit, gr...]
where the time goes in v9:
time: 47 us; the launch traced here: 46.9 us
  Pallas kernels  45.1 us (96%)
  local copies, waits for them, and re-layouts  1.08 us (2%)
  between operations  0.65 us (1%)
    pallas_call x1, Pallas kernels, body(): pl.pallas_call(functools.partial(exchange_kernel, parts, blocks, unit, gr...  42.7 us
    pallas_call x1, Pallas kernels, body(): pl.pallas_call(functools.partial(gram_kernel, rows ** (-0.5), width, earl...  2.48 us
    unnamed x2, local copies, waits for them, and re-layouts  1.08 us

profile of v9, /device:TPU:0, one launch (start us, length us, event | category | flops | bytes accessed | tf_op | source)
XLA Modules:
  0.0 46.9 jit_solution(255683254863059269)
XLA Ops:
  0.6 0.0 copy-start
  0.6 1.1 %copy-done = bf16[16,160,128]{2,1,0:T(8,128)(2,1)S(1)} copy-done((bf16[16,160,128]{2,1,0:T(8,128)(2,1)S(1)}, bf16[16,160,128]{2,1,0:T(8,128)(2,1)}, u32[]{:S(2)}) %copy-start) | copy-done | bytes 655384
  1.7 42.7 %exchange.1 = (f32[8,2,128,256]{3,2,1,0:T(8,128)S(1)}, bf16[16,80,256]{2,1,0:T(8,128)(2,1)S(1)}) custom-call(bf16[16,160,128]{2,1,0:T(8,128)(2,1)S(1)} %copy-done), custom_call_target="tpu_custom_call" | custom-call | tf_op jit(solution)/shard_map/exchange/pallas_call | solution.py:330
  44.4 2.5 %grams.1 = (f32[8,2,128,256]{3,2,1,0:T(8,128)}, f32[8,2,128,256]{3,2,1,0:T(8,128)}) custom-call(f32[8,2,128,256]{3,2,1,0:T(8,128)S(1)} %get-tuple-element.4.refs_0_, bf16[16,80,256]{2,1,0:T(8,128)(2,1)S(1)} %get-tuple-element.5.refs_1_), custom_call_target="tpu_custom_call" | custom-call | tf_op jit(solution)/shard_map/grams/pallas_call | solution.py:352
Async XLA Ops:
  0.6 1.1 %copy-start = (bf16[16,160,128]{2,1,0:T(8,128)(2,1)S(1)}, bf16[16,160,128]{2,1,0:T(8,128)(2,1)}, u32[]{:S(2)}) copy-start(bf16[16,160,128]{2,1,0:T(8,128)(2,1)} %x_ref.1) | copy-start | bytes 1966084

commit v10 on v9

--- a/solution.py
+++ b/solution.py
@@ -125,7 +125,7 @@
             src_ref=tx.at[c, to],
             dst_ref=rx2.at[tm, c, me],
             send_sem=send2.at[c],
-            recv_sem=recv2.at[c, s],
+            recv_sem=recv2.at[c, s if c == chunks - 1 else 0],
             device_id=(tm, to),
             device_id_type=MESH,
         )
@@ -205,7 +205,8 @@
                 tx[c, :, q * unit:(q + 1) * unit, :] = out.reshape(parts, unit, width)
         loop(lambda s, c=c: copy2(c, s).start())
         rx2[tm, c, me] = tx[c, me]
-        forward(c, me)
+        if c == chunks - 1:
+            forward(c, me)
 
     span = padded // chunks
 
@@ -263,8 +264,12 @@
             for m in range(per_set):
                 early_gram(m)
                 loop(pass_on, head + rest * m // per_set, head + rest * (m + 1) // per_set)
+        elif c == chunks - 1:
+            loop(pass_on)
         else:
-            loop(pass_on)
+            all2(c).wait_recv()
+            for d in range(1, blocks):
+                guarded(needed_by(d), lambda c=c, d=d: all3(c, d, tm).start())
         regroup(tm, c)
     for c in range(chunks):
         all1(c).wait_send()

time: 47 us -> 51 us (1.085); the launches traced: 46.9 us -> 50.2 us
  Pallas kernels: 45.1 us -> 48.5 us
    pallas_call x1, Pallas kernels: 42.7 us -> 46 us  [body(): pl.pallas_call(functools.partial(exchange_kernel, parts, blocks, unit, gr...]
where the time goes in v10:
time: 51 us; the launch traced here: 50.2 us
  Pallas kernels  48.5 us (95%)
  local copies, waits for them, and re-layouts  1.08 us (2%)
  between operations  0.65 us (1%)
    pallas_call x1, Pallas kernels, body(): pl.pallas_call(functools.partial(exchange_kernel, parts, blocks, unit, gr...  46 us
    pallas_call x1, Pallas kernels, body(): pl.pallas_call(functools.partial(gram_kernel, rows ** (-0.5), width, earl...  2.48 us
    unnamed x2, local copies, waits for them, and re-layouts  1.08 us

profile of v10, /device:TPU:0, one launch (start us, length us, event | category | flops | bytes accessed | tf_op | source)
XLA Modules:
  0.0 50.2 jit_solution(10246359690852285973)
XLA Ops:
  0.6 0.0 copy-start
  0.6 1.1 %copy-done = bf16[16,160,128]{2,1,0:T(8,128)(2,1)S(1)} copy-done((bf16[16,160,128]{2,1,0:T(8,128)(2,1)S(1)}, bf16[16,160,128]{2,1,0:T(8,128)(2,1)}, u32[]{:S(2)}) %copy-start) | copy-done | bytes 655384
  1.7 46.0 %exchange.1 = (f32[8,2,128,256]{3,2,1,0:T(8,128)S(1)}, bf16[16,80,256]{2,1,0:T(8,128)(2,1)S(1)}) custom-call(bf16[16,160,128]{2,1,0:T(8,128)(2,1)S(1)} %copy-done), custom_call_target="tpu_custom_call" | custom-call | tf_op jit(solution)/shard_map/exchange/pallas_call | solution.py:335
  47.7 2.5 %grams.1 = (f32[8,2,128,256]{3,2,1,0:T(8,128)}, f32[8,2,128,256]{3,2,1,0:T(8,128)}) custom-call(f32[8,2,128,256]{3,2,1,0:T(8,128)S(1)} %get-tuple-element.4.refs_0_, bf16[16,80,256]{2,1,0:T(8,128)(2,1)S(1)} %get-tuple-element.5.refs_1_), custom_call_target="tpu_custom_call" | custom-call | tf_op jit(solution)/shard_map/grams/pallas_call | solution.py:357
Async XLA Ops:
  0.6 1.1 %copy-start = (bf16[16,160,128]{2,1,0:T(8,128)(2,1)S(1)}, bf16[16,160,128]{2,1,0:T(8,128)(2,1)}, u32[]{:S(2)}) copy-start(bf16[16,160,128]{2,1,0:T(8,128)(2,1)} %x_ref.1) | copy-start | bytes 1966084
